TPU v7x, 512 devices: a whole 4x4x16 slice. The times are simulated.
512 devices in a mesh: dp: 128 (over x, z, core), mp: 4 (over y).
Axes of the slice: x: 4, y: 4, z: 16, core: 2. Of those that a mesh axis runs over, the one named last changes fastest.
Arguments:
- frames: bfloat16 [32768, 1536], P('dp')
- lengths: int32 [128], P('dp'), may hold values from 32 to 256
- send_order: int32 [128, 256], P('dp'), may hold values from 0 to 255, each once within a row
- value_weight: bfloat16 [1536, 768], P('dp', 'mp'), may hold values from -0.15625 to 0.15625
- gate_weight: bfloat16 [1536, 768], P('dp', 'mp'), may hold values from -0.15625 to 0.15625
- down_weight: bfloat16 [1536, 768], P('dp', 'mp'), may hold values from -0.21875 to 0.21875
- cotangent: bfloat16 [32768, 1536], P('dp'), may hold values from -0.125 to 0.125
Outputs:
- branch: bfloat16 [32768, 1536], P('dp')
- grad_value: float32 [1536, 768], P('dp', 'mp')
- grad_gate: float32 [1536, 768], P('dp', 'mp')
- grad_down: float32 [1536, 768], P('dp', 'mp')
All inputs are finite; a program needn't handle non-finite values.
Results may differ from a plain program's by a relative error of at most 0.0059.
Values may be sent and summed in bfloat16 or wider, within the bound.
A program may use at most 64 MiB of HBM per device.

v0:
```python
import jax
import jax.numpy as jnp
from jax import lax
from jax.sharding import PartitionSpec as P


def contract_rows(left, right):
    return lax.dot_general(
        left, right, (((0,), (0,)), ((), ())), preferred_element_type=jnp.float32
    )


def contract_cols(left, right):
    return lax.dot_general(
        left, right, (((1,), (1,)), ((), ())), preferred_element_type=jnp.float32
    )


def shards(frames, lengths, send_order, value_weight, gate_weight, down_weight, cotangent):
    rows_here = frames.shape[0]
    utterances = lengths.shape[0]
    slot_len = rows_here // utterances
    position = lax.broadcasted_iota(jnp.int32, (utterances, slot_len), 1)
    live = (position < lengths[:, None]).reshape(rows_here, 1)
    masked = jnp.where(live, frames, jnp.zeros_like(frames))
    outgoing = jnp.take(masked, send_order.reshape(-1), axis=0)
    moved = lax.all_to_all(outgoing, "dp", split_axis=0, concat_axis=0, tiled=True)
    values_w, gates_w, downs_w = (
        lax.all_gather(value_weight, "dp", axis=0, tiled=True),
        lax.all_gather(gate_weight, "dp", axis=0, tiled=True),
        lax.all_gather(down_weight, "dp", axis=0, tiled=True),
    )
    wide = moved.astype(jnp.float32)
    mean = jnp.mean(wide, axis=1, keepdims=True)
    var = jnp.mean(jnp.square(wide - mean), axis=1, keepdims=True)
    normed = ((wide - mean) * lax.rsqrt(var + 1e-05)).astype(jnp.bfloat16)
    value = jnp.dot(normed, values_w, preferred_element_type=jnp.float32)
    gate = jnp.dot(normed, gates_w, preferred_element_type=jnp.float32)
    sig = jax.nn.sigmoid(gate)
    glu = (value * sig).astype(jnp.bfloat16)
    partial_out = contract_cols(glu, downs_w)
    branch = lax.psum(partial_out, "mp").astype(jnp.bfloat16)
    dglu = jnp.dot(cotangent, downs_w, preferred_element_type=jnp.float32)
    d_value = (dglu * sig).astype(jnp.bfloat16)
    d_gate = (dglu * value * sig * (1.0 - sig)).astype(jnp.bfloat16)
    units = glu.shape[1]
    owned = lax.psum_scatter(
        jnp.concatenate(
            [
                contract_rows(normed, d_value),
                contract_rows(normed, d_gate),
                contract_rows(cotangent, glu),
            ],
            axis=1,
        ),
        "dp",
        scatter_dimension=0,
        tiled=True,
    )
    grad_value = owned[:, :units]
    grad_gate = owned[:, units : 2 * units]
    grad_down = owned[:, 2 * units :]
    return (branch, grad_value, grad_gate, grad_down)


def solution(mesh):
    return jax.shard_map(
        shards,
        mesh=mesh,
        in_specs=(
            P("dp", None),
            P("dp"),
            P("dp", None),
            P("dp", "mp"),
            P("dp", "mp"),
            P("dp", "mp"),
            P("dp", None),
        ),
        out_specs=(P("dp", None), P("dp", "mp"), P("dp", "mp"), P("dp", "mp")),
        check_vma=False,
    )
```

profile of v0, /device:TPU:1, one launch (start us, length us, event | category | flops | bytes accessed | tf_op | source)
XLA Modules:
  0.0 743.2 jit_solution(2838817702133727190)
XLA Ops:
  7.2 0.0 copy-start
  7.9 0.7 compare_select_fusion.1
  8.6 1.3 broadcast_select_fusion.1
  9.9 1.3 gather_fusion
  11.1 0.0 copy-start.6
  11.1 0.3 gather.7
  11.4 0.5 broadcast.85
  12.0 0.0 copy-done.6
  12.0 0.7 reduce.5
  12.6 0.1 reshape.99
  12.8 0.0 copy-start.3
  12.8 1.7 broadcast_select_fusion
  14.5 20.4 %all-to-all-start = ((bf16[128,2,1536]{2,1,0:T(2,128)(2,1)}), bf16[128,2,1536]{2,1,0:T(2,128)(2,1)S(1)}, u32[]{:S(2)}, u32[]{:S(2)}) async-start(bf16[128,2,1536]{2,1,0:T(2,128)(2,1)} %broadcast_select_fusion), calls=%async_computation | async-start | bytes 1572864 | tf_op jit(solution)/shard_map/all_to_all | solution.py:27
  34.9 0.0 copy-start.4
  34.9 0.0 all-reduce.4.cloned.1.call-start
  35.0 0.0 copy-done.3
  35.0 131.0 %all-gather.1 = bf16[128,12,192]{2,1,0:T(8,128)(2,1)S(1)} all-gather(bf16[1,12,192]{2,1,0:T(8,128)(2,1)S(1)} %bitcast.25), channel_id=1, replica_groups=mesh['dp'=128,'mp'=4] {'dp'}, dimensions={0}, use_global_device_ids=true | all-gather | bytes 594432 | tf_op jit(solution)/shard_map/all_gather | solution.py:30
  166.0 1.3 reshape.113
  167.3 0.0 copy-done.4
  167.3 100.1 %all-gather = bf16[128,12,192]{2,1,0:T(8,128)(2,1)S(1)} all-gather(bf16[1,12,192]{2,1,0:T(8,128)(2,1)S(1)} %bitcast.26), channel_id=1, replica_groups=mesh['dp'=128,'mp'=4] {'dp'}, dimensions={0}, use_global_device_ids=true | all-gather | bytes 594432 | tf_op jit(solution)/shard_map/all_gather | solution.py:29
  267.5 1.3 reshape.111
  268.8 0.0 copy-done.5
  268.8 98.2 %all-gather.2 = bf16[128,12,192]{2,1,0:T(8,128)(2,1)S(1)} all-gather(bf16[1,12,192]{2,1,0:T(8,128)(2,1)S(1)} %bitcast.27), channel_id=1, replica_groups=mesh['dp'=128,'mp'=4] {'dp'}, dimensions={0}, use_global_device_ids=true | all-gather | bytes 594432 | tf_op jit(solution)/shard_map/all_gather | solution.py:31
  367.0 0.4 reshape.115
  367.4 1.3 dynamic-slice
  369.4 0.5 fusion.9
  369.8 0.0 all-to-all-done
  369.9 0.7 convert_reduce_fusion
  370.5 0.1 div.12
  370.7 1.2 multiply_reduce_fusion
  371.9 0.1 rsqrt.12
  372.0 1.4 reshape.101
  373.4 1.7 multiply_convert_fusion
  375.1 0.4 fusion.2
  375.6 0.7 copy-done.1
  376.3 0.5 multiply_convert_fusion.3
  376.8 0.3 fusion.3
  377.1 0.3 fusion.4
  377.4 0.3 convolution_bitcast_fusion
  377.7 2.0 pad_maximum_fusion
  379.8 0.0 all-reduce.4.cloned.1.call-update
  379.8 0.4 fusion.8
  380.2 33.6 %all-reduce.5 = bf16[256,1536]{1,0:T(8,128)(2,1)} all-reduce(f32[256,1536]{1,0:T(8,128)S(1)} %fusion.8), channel_id=1, replica_groups=mesh['dp'=128,'mp'=4] {'mp'}, use_global_device_ids=true, to_apply=%region_2.3 | all-reduce | flops 393216 | bytes 2359296 | tf_op jit(solution)/shard_map/psum | solution.py:42
  413.8 319.3 %all-reduce.4.cloned.1.call-done = f32[1536,576]{0,1:T(8,128)} async-done(((f32[1536,576]{0,1:T(8,128)}), f32[1536,576]{0,1:T(8,128)}) %all-reduce.4.cloned.1.call-update) | async-done | bytes 3538960
  733.0 1.3 fusion.7
  734.3 0.7 copy.17
  735.0 0.7 copy.18
  735.7 0.7 copy.19
  (10 shorter events, 0.1 us)
Async XLA Ops:
  7.2 362.2 %copy-start = (bf16[256,1536]{1,0:T(8,128)(2,1)S(1)}, bf16[256,1536]{1,0:T(8,128)(2,1)}, u32[]{:S(2)}) copy-start(bf16[256,1536]{1,0:T(8,128)(2,1)} %param.13) | copy-start | bytes 2359300
  11.1 0.8 copy-start.6
  12.8 22.2 %copy-start.3 = (bf16[12,192]{1,0:T(8,128)(2,1)S(1)}, bf16[12,192]{1,0:T(8,128)(2,1)}, u32[]{:S(2)}) copy-start(bf16[12,192]{1,0:T(8,128)(2,1)} %param.11) | copy-start | bytes 13828
  14.5 355.3 %all-to-all-start = ((bf16[128,2,1536]{2,1,0:T(2,128)(2,1)}), bf16[128,2,1536]{2,1,0:T(2,128)(2,1)S(1)}, u32[]{:S(2)}, u32[]{:S(2)}) async-start(bf16[128,2,1536]{2,1,0:T(2,128)(2,1)} %broadcast_select_fusion), calls=%async_computation | async-start | bytes 1572864 | tf_op jit(solution)/shard_map/all_to_all | solution.py:27
  34.9 132.4 %copy-start.4 = (bf16[12,192]{1,0:T(8,128)(2,1)S(1)}, bf16[12,192]{1,0:T(8,128)(2,1)}, u32[]{:S(2)}) copy-start(bf16[12,192]{1,0:T(8,128)(2,1)} %param.10) | copy-start | bytes 13828
  34.9 698.1 %all-reduce.4.cloned.1.call-start = ((), (), s32[]{:S(2)}) async-start(), calls=%async_computation.1 | async-start | bytes 7077888
  167.3 101.5 %copy-start.5 = (bf16[12,192]{1,0:T(8,128)(2,1)S(1)}, bf16[12,192]{1,0:T(8,128)(2,1)}, u32[]{:S(2)}) copy-start(bf16[12,192]{1,0:T(8,128)(2,1)} %param.12) | copy-start | bytes 13828
  373.4 1.7 copy-start.2
  375.1 1.1 copy-start.1
Sparse Core Ops, SparseCore 0:
  379.9 353.0 all-reduce.3
where the time goes:
time: 745 us; the launch traced here: 743 us
  blocking collectives  363 us (49%)
  waiting for transfers between devices  319 us (43%)
  starting transfers between devices  20.4 us (3%)
  between operations  15.6 us (2%)
  local copies, waits for them, and re-layouts  12.2 us (2%)
  other arithmetic  9.98 us (1%)
    unnamed x2, waiting for transfers between devices  319 us
    all_gather x1, blocking collectives, shards(): lax.all_gather(gate_weight, 'dp', axis=0, tiled=True)  131 us
    all_gather x1, blocking collectives, shards(): lax.all_gather(value_weight, 'dp', axis=0, tiled=True)  100 us
    all_gather x1, blocking collectives, shards(): lax.all_gather(down_weight, 'dp', axis=0, tiled=True)  98.2 us
    psum x1, blocking collectives, shards(): branch = lax.psum(partial_out, 'mp').astype(jnp.bfloat16)  33.6 us
    all_to_all x1, starting transfers between devices, shards(): lax.all_to_all(outgoing, 'dp', split_axis=0, concat_axis=0, tiled=True)  20.4 us
  transfers between devices with their start and end apart: 2, of which 1 were waited for; matrix products, arithmetic and copies ran while one was open for 1% of the time, Pallas kernels for 0%

commit v1 on v0

v1 whole, which is shorter than its diff:
```python
import functools

import jax
import jax.numpy as jnp
from jax import lax
from jax.experimental import pallas as pl
from jax.experimental.pallas import tpu as pltpu
from jax.sharding import PartitionSpec as P

CORES = 2
BF = jnp.bfloat16
F32 = jnp.float32


def ceil16(rows):
    return -(-rows // 16) * 16


def iota(shape, axis):
    return lax.broadcasted_iota(jnp.int32, shape, axis)


def onehot(hit):
    return jnp.where(hit, 1.0, 0.0).astype(BF)


def dot(left, right):
    return jnp.dot(left, right, preferred_element_type=F32)


def contract_rows(left, right):
    return lax.dot_general(left, right, (((0,), (0,)), ((), ())), preferred_element_type=F32)


def contract_cols(left, right):
    return lax.dot_general(left, right, (((1,), (1,)), ((), ())), preferred_element_type=F32)


def mod(value, count):
    return lax.rem(value + count, count)


class Sizes:
    def __init__(self, X, Z, Y, rows, width, own, units):
        self.X, self.Z, self.Y = X, Z, Y
        self.G = X * CORES
        self.rows, self.width, self.own, self.units = rows, width, own, units
        self.cap = rows // (X * Z * CORES)
        self.part = width // Y
        self.pad = ceil16(own)
        self.zrow = self.G * self.cap
        self.grow = self.Z * self.cap
        self.zw = self.G * own
        self.pair = CORES * own
        self.pairpad = ceil16(self.pair)
        self.cols = 3 * units
        self.half = Z // 2 * self.pair
        self.yrow = rows // Y


def kernel(
    cfg,
    lengths, send_order, frames, value_w, gate_w, down_w, cotangent,
    branch, grad_value, grad_gate, grad_down,
    out1, in1, out2, moved_parts, wide, normed,
    pack, shards, slots, weights,
    grads, pair_out, pair_in, sums, x1_out, x1_in, x2_out, x2_in, mine, z_out, z_in, final,
    terms, y1_out, y1_in, y2_out, y2_in, result,
    s_w1, r_w1, s_ring, r_ring, s_sib, r_sib,
    s_a1, r_a1, s_a2, r_a2, s_ag, r_ag,
    s_pair, r_pair, s_x, r_x, s_z, r_z, s_fin, r_fin, s_y, r_y,
):
    X, Z, Y, G = cfg.X, cfg.Z, cfg.Y, cfg.G
    U = cfg.units
    dp = lax.axis_index("dp")
    y = lax.axis_index("mp")
    core = lax.rem(dp, CORES)
    z = lax.rem(lax.div(dp, CORES), Z)
    x = lax.div(dp, CORES * Z)
    g = x * CORES + core
    other = 1 - core

    def at(x_, z_, core_, y_=None):
        return {"dp": (x_ * Z + z_) * CORES + core_, "mp": y if y_ is None else y_}

    def remote(src, dst, send, recv, where):
        return pltpu.make_async_remote_copy(
            src_ref=src, dst_ref=dst, send_sem=send, recv_sem=recv,
            device_id=where, device_id_type=pl.DeviceIdType.MESH,
        )

    def rows_of(ref, start, size, step=16):
        return ref.at[pl.ds(pl.multiple_of(start, step), size)]

    sibling = at(x, z, other)
    y_up, y_down = at(x, z, core, mod(y + 1, Y)), at(x, z, core, mod(y - 1, Y))
    x_up, x_down = at(mod(x + 1, X), z, core), at(mod(x - 1, X), z, core)

    barrier = pltpu.get_barrier_semaphore()
    partners = []
    for o in range(1, G):
        t = mod(g + o, G)
        partners.append(at(lax.div(t, CORES), z, lax.rem(t, CORES)))
    for o in range(1, Z):
        partners.append(at(x, mod(z + o, Z), core))
    partners += [y_up, y_down]
    for who in partners:
        pl.semaphore_signal(barrier, inc=1, device_id=who, device_id_type=pl.DeviceIdType.MESH)

    packed = jnp.concatenate([value_w[...], gate_w[...], down_w[...]], axis=1)
    pack[...] = jnp.zeros_like(pack)
    pack[0 : cfg.own, :] = packed

    R = cfg.rows
    r_nat, r_new = iota((R, R), 0), iota((R, R), 1)
    k_new = lax.rem(r_new, cfg.cap)
    z_new = lax.rem(lax.div(r_new, cfg.cap), Z)
    g_new = lax.div(r_new, cfg.cap * Z)
    natural = ((lax.div(g_new, CORES) * Z + z_new) * CORES + lax.rem(g_new, CORES)) * cfg.cap + k_new
    to_dest = onehot(r_nat == natural)
    order = dot(jnp.broadcast_to(send_order[...].astype(F32).astype(BF), (16, R)), to_dest)[0:1, :]
    slot = iota((R, R), 0)
    pick = onehot((slot.astype(F32) == order) & (slot < lengths[0]))
    columns = pl.ds(pl.multiple_of(y * cfg.part, 128), cfg.part)
    out1[...] = contract_rows(pick, frames[:, columns]).astype(BF)

    pl.semaphore_wait(barrier, len(partners))

    w1, a1 = [], []
    for o in range(1, G):
        t = mod(g + o, G)
        where = at(lax.div(t, CORES), z, lax.rem(t, CORES))
        w1.append(remote(pack, rows_of(shards, g * cfg.pad, cfg.pad), s_w1.at[o], r_w1.at[o], where))
        w1[-1].start()
        a1.append(remote(
            rows_of(out1, t * cfg.grow, cfg.grow), rows_of(in1, g * cfg.grow, cfg.grow),
            s_a1.at[o], r_a1.at[o], where,
        ))
        a1[-1].start()
    rows_of(shards, g * cfg.pad, cfg.pad)[...] = pack[...]
    rows_of(in1, g * cfg.grow, cfg.grow)[...] = rows_of(out1, g * cfg.grow, cfg.grow)[...]

    for copy in w1:
        copy.wait_recv()
    i_new, i_old = iota((cfg.zw, G * cfg.pad), 0), iota((cfg.zw, G * cfg.pad), 1)
    j_old = lax.rem(i_old, cfg.pad)
    squeeze = onehot((j_old < cfg.own) & (lax.div(i_old, cfg.pad) * cfg.own + j_old == i_new))
    slots[z] = dot(squeeze, shards[...]).astype(BF)

    way = 1 - 2 * core
    ring_to = at(x, mod(z + way, Z), core)
    last = Z // 2 - 1
    half_w = cfg.zw // 2

    def slot_ref(step, sign):
        ref = slots.at[mod(z - sign * way * step, Z)]
        return ref

    def half_ref(step, part):
        return rows_of(slots.at[mod(z - way * step, Z)], part * half_w, half_w)

    ring, sib = [], []

    def ring_send(step):
        if step < last:
            ref = slot_ref(step, 1)
        else:
            ref = half_ref(step, core)
        ring.append(remote(ref, ref, s_ring.at[step], r_ring.at[step], ring_to))
        ring[-1].start()

    def ring_take(step):
        ring[step].wait_recv()
        if step < last:
            ref = slot_ref(step + 1, 1)
        else:
            ref = half_ref(step + 1, core)
        if step < last:
            ring_send(step + 1)
        sib.append(remote(ref, ref, s_sib.at[step], r_sib.at[step], sibling))
        sib[-1].start()

    ring_send(0)

    for copy in a1:
        copy.wait_recv()
    r_new, r_old = iota((R, R), 0), iota((R, R), 1)
    k_new = lax.rem(r_new, cfg.cap)
    g_new = lax.rem(lax.div(r_new, cfg.cap), G)
    z_new = lax.div(r_new, cfg.zrow)
    out2[...] = dot(onehot(r_old == (g_new * Z + z_new) * cfg.cap + k_new), in1[...]).astype(BF)
    a2 = []
    for o in range(1, Z):
        t = mod(z + o, Z)
        a2.append(remote(
            rows_of(out2, t * cfg.zrow, cfg.zrow), rows_of(moved_parts.at[y], z * cfg.zrow, cfg.zrow),
            s_a2.at[o], r_a2.at[o], at(x, t, core),
        ))
        a2[-1].start()
    rows_of(moved_parts.at[y], z * cfg.zrow, cfg.zrow)[...] = rows_of(out2, z * cfg.zrow, cfg.zrow)[...]

    for step in range(last):
        ring_take(step)

    for copy in a2:
        copy.wait_recv()

    ag = []
    for i, where in enumerate((y_up, y_down)):
        ag.append(remote(moved_parts.at[y], moved_parts.at[y], s_ag.at[i], r_ag.at[i], where))
        ag[-1].start()

    ring_take(last)

    for copy in ag[:2]:
        copy.wait_recv()
    for i, where in enumerate((y_up, y_down)):
        ref = rows_of(moved_parts.at[mod(y - 1 + 2 * i, Y)], i * (R // 2), R // 2)
        ag.append(remote(ref, ref, s_ag.at[2 + i], r_ag.at[2 + i], where))
        ag[-1].start()

    for copy in sib:
        copy.wait_recv()
    for xi in range(X):
        pieces = [
            slots[zi].astype(F32)[xi * cfg.pair : (xi + 1) * cfg.pair] for zi in range(Z)
        ]
        weights[xi * Z * cfg.pair : (xi + 1) * Z * cfg.pair, :] = jnp.concatenate(pieces, axis=0).astype(BF)

    dglu = dot(cotangent[...], weights[:, 2 * U : 3 * U])

    for copy in ag[2:]:
        copy.wait_recv()

    r_new, r_old = iota((R, R), 0), iota((R, R), 1)
    k_new = lax.rem(r_new, cfg.cap)
    c_new = lax.rem(lax.div(r_new, cfg.cap), CORES)
    z_new = lax.rem(lax.div(r_new, cfg.cap * CORES), Z)
    x_new = lax.div(r_new, cfg.cap * CORES * Z)
    back = onehot(r_old == ((z_new * X + x_new) * CORES + c_new) * cfg.cap + k_new)
    for q in range(Y):
        wide[:, q * cfg.part : (q + 1) * cfg.part] = dot(back, moved_parts[q])
    lines = 32
    for i in range(R // lines):
        block = wide[i * lines : (i + 1) * lines, :]
        mean = jnp.mean(block, axis=1, keepdims=True)
        centred = block - mean
        var = jnp.mean(jnp.square(centred), axis=1, keepdims=True)
        normed[i * lines : (i + 1) * lines, :] = (centred * lax.rsqrt(var + 1e-05)).astype(BF)

    both = dot(normed[...], weights[:, : 2 * U])
    value, gate = both[:, :U], both[:, U : 2 * U]
    sig = jax.nn.sigmoid(gate)
    glu = (value * sig).astype(BF)
    d_value = (dglu * sig).astype(BF)
    d_gate = (dglu * value * sig * (1.0 - sig)).astype(BF)

    grads[:, : 2 * U] = contract_rows(normed[...], jnp.concatenate([d_value, d_gate], axis=1))
    grads[:, 2 * U :] = contract_rows(cotangent[...], glu)
    span = Z * cfg.pair
    pairs = {}
    for o in (2, 1, 3, 0):
        t = mod(x + o, X)
        pair_out[t] = rows_of(grads, t * span + other * cfg.half, cfg.half)[...].astype(BF)
        pairs[o] = remote(pair_out.at[t], pair_in.at[t], s_pair.at[o], r_pair.at[o], sibling)
        pairs[o].start()

    B = cfg.yrow
    terms[...] = contract_cols(glu, weights[:, 2 * U : 3 * U])
    far = rows_of(terms, mod(y + 2, Y) * B, B)
    y1_out[...] = far[...].astype(BF)
    y1 = []
    for i, where in enumerate((y_up, y_down)):
        y1.append(remote(
            y1_out.at[i * (B // 2) : (i + 1) * (B // 2)], y1_in.at[i], s_y.at[i], r_y.at[i], where,
        ))
        y1[-1].start()

    def paired(o):
        t = mod(x + o, X)
        pairs[o].wait_recv()
        sums[o] = rows_of(grads, t * span + core * cfg.half, cfg.half)[...] + pair_in[t].astype(F32)

    S = cfg.half
    paired(2)
    x1_out[...] = sums[2].astype(BF)
    x1 = []
    for i, where in enumerate((x_up, x_down)):
        x1.append(remote(
            x1_out.at[i * (S // 2) : (i + 1) * (S // 2)], x1_in.at[i], s_x.at[i], r_x.at[i], where,
        ))
        x1[-1].start()
    paired(1)
    paired(3)
    paired(0)

    y2 = []
    for i, where in enumerate((y_up, y_down)):
        y1[i].wait_recv()
        mid = rows_of(terms, mod(y + 1 - 2 * i, Y) * B, B)
        mid[i * (B // 2) : (i + 1) * (B // 2), :] = (
            mid[i * (B // 2) : (i + 1) * (B // 2), :] + y1_in[i].astype(F32)
        )
        y2_out[i] = mid[...].astype(BF)
        y2.append(remote(y2_out.at[i], y2_in.at[i], s_y.at[2 + i], r_y.at[2 + i], where))
        y2[-1].start()

    x2 = []
    for i, where in enumerate((x_up, x_down)):
        x1[i].wait_recv()
        lo, hi = i * (S // 2), (i + 1) * (S // 2)
        sums[1 + 2 * i, lo:hi, :] = sums[1 + 2 * i, lo:hi, :] + x1_in[i].astype(F32)
        x2_out[i] = sums[1 + 2 * i].astype(BF)
        x2.append(remote(x2_out.at[i], x2_in.at[i], s_x.at[2 + i], r_x.at[2 + i], where))
        x2[-1].start()

    for copy in y2:
        copy.wait_recv()
    own_rows = (
        rows_of(terms, y * B, B)[...] + y2_in[0].astype(F32) + y2_in[1].astype(F32)
    )
    rows_of(result, y * B, B)[...] = own_rows.astype(BF)
    yg = []
    for i, where in enumerate((y_up, y_down)):
        ref = rows_of(result, y * B, B)
        yg.append(remote(ref, ref, s_y.at[4 + i], r_y.at[4 + i], where))
        yg[-1].start()

    for copy in x2:
        copy.wait_recv()
    mine[...] = sums[0] + x2_in[0].astype(F32) + x2_in[1].astype(F32)
    Q = cfg.pair
    z_out[...] = jnp.zeros_like(z_out)
    zs = []
    for i in range(Z // 2):
        z_out[i, 0:Q, :] = mine[i * Q : (i + 1) * Q, :].astype(BF)
        t = core * (Z // 2) + i
        zs.append((t != z, remote(z_out.at[i], z_in.at[z], s_z.at[i], r_z.at[z], at(x, t, core))))
        pl.when(t != z)(zs[-1][1].start)

    for copy in yg[:2]:
        copy.wait_recv()
    for i, where in enumerate((y_up, y_down)):
        ref = rows_of(result, mod(y - 1 + 2 * i, Y) * B + i * (B // 2), B // 2)
        yg.append(remote(ref, ref, s_y.at[6 + i], r_y.at[6 + i], where))
        yg[-1].start()

    hand = remote(final, final, s_fin.at[0], r_fin.at[0], sibling)
    is_owner = lax.div(z, Z // 2) == core

    @pl.when(is_owner)
    def _():
        for o in range(1, Z):
            t = mod(z + o, Z)
            remote(z_out.at[0], z_in.at[t], s_z.at[0], r_z.at[t], sibling).wait_recv()
        total = rows_of(mine, (z - core * (Z // 2)) * Q, Q, 8)[...]
        for o in range(1, Z):
            total = total + z_in[mod(z + o, Z)][0:Q].astype(F32)
        final[...] = total
        hand.start()
        hand.wait_send()

    @pl.when(jnp.logical_not(is_owner))
    def _():
        hand.wait_recv()

    whole = final[...]
    owned = jnp.where(core == 0, whole[0 : cfg.own], whole[cfg.own : 2 * cfg.own])
    grad_value[...] = owned[:, :U]
    grad_gate[...] = owned[:, U : 2 * U]
    grad_down[...] = owned[:, 2 * U :]

    for copy in yg[2:]:
        copy.wait_recv()
    branch[...] = result[...]

    for copy in w1 + a1 + ring + sib + a2 + ag + list(pairs.values()) + y1 + x1 + y2 + x2 + yg:
        copy.wait_send()
    for needed, copy in zs:
        pl.when(needed)(copy.wait_send)


def module(cfg, frames, lengths, send_order, value_weight, gate_weight, down_weight, cotangent):
    X, Z, Y, G, R, D, U = cfg.X, cfg.Z, cfg.Y, cfg.G, cfg.rows, cfg.width, cfg.units
    C, S, B = cfg.cols, cfg.half, cfg.yrow
    vmem = pl.BlockSpec(memory_space=pltpu.VMEM)
    sem = pltpu.SemaphoreType.DMA
    buffers = [
        ((R, cfg.part), BF),
        ((R, cfg.part), BF),
        ((R, cfg.part), BF),
        ((Y, R, cfg.part), BF),
        ((R, D), F32),
        ((R, D), BF),
        ((cfg.pad, C), BF),
        ((G * cfg.pad, C), BF),
        ((Z, cfg.zw, C), BF),
        ((D, C), BF),
        ((D, C), F32),
        ((X, S, C), BF),
        ((X, S, C), BF),
        ((X, S, C), F32),
        ((S, C), BF),
        ((2, S // 2, C), BF),
        ((2, S, C), BF),
        ((2, S, C), BF),
        ((S, C), F32),
        ((Z // 2, cfg.pairpad, C), BF),
        ((Z, cfg.pairpad, C), BF),
        ((cfg.pair, C), F32),
        ((R, D), F32),
        ((B, D), BF),
        ((2, B // 2, D), BF),
        ((2, B, D), BF),
        ((2, B, D), BF),
        ((R, D), BF),
    ]
    sems = [G, Z // 2, Z // 2, G, Z, 4, X, 4, Z, 1, 8]
    return pl.pallas_call(
        functools.partial(kernel, cfg),
        out_shape=(
            jax.ShapeDtypeStruct((R, D), BF),
            jax.ShapeDtypeStruct((cfg.own, U), F32),
            jax.ShapeDtypeStruct((cfg.own, U), F32),
            jax.ShapeDtypeStruct((cfg.own, U), F32),
        ),
        in_specs=[pl.BlockSpec(memory_space=pltpu.SMEM)] + [vmem] * 6,
        out_specs=(vmem,) * 4,
        scratch_shapes=[pltpu.VMEM(shape, kind) for shape, kind in buffers]
        + [sem((n,)) for n in sems for _ in range(2)],
        compiler_params=pltpu.CompilerParams(
            collective_id=0, has_side_effects=True, vmem_limit_bytes=56 * 1024 * 1024
        ),
    )(lengths, send_order, frames, value_weight, gate_weight, down_weight, cotangent)


def build(mesh, X, Z):
    def shards(frames, lengths, send_order, value_weight, gate_weight, down_weight, cotangent):
        cfg = Sizes(
            X, Z, mesh.shape["mp"], frames.shape[0], frames.shape[1],
            value_weight.shape[0], value_weight.shape[1],
        )
        return module(
            cfg, frames, lengths, send_order, value_weight, gate_weight, down_weight, cotangent
        )

    return jax.shard_map(
        shards,
        mesh=mesh,
        in_specs=(
            P("dp", None),
            P("dp"),
            P("dp", None),
            P("dp", "mp"),
            P("dp", "mp"),
            P("dp", "mp"),
            P("dp", None),
        ),
        out_specs=(P("dp", None), P("dp", "mp"), P("dp", "mp"), P("dp", "mp")),
        check_vma=False,
    )


def solution(mesh):
    return build(mesh, 4, 16)
```

time: 745 us -> 107 us (0.14)
  blocking collectives: 363 us -> 0 us
  waiting for transfers between devices: 319 us -> 0 us
  Pallas kernels: 0 us -> 101 us
  starting transfers between devices: 20.4 us -> 0 us
  between operations: 15.6 us -> 1.3 us
  other arithmetic: 9.98 us -> 0 us
  local copies, waits for them, and re-layouts: 12.2 us -> 4.13 us
    all_gather x3 -> x0, blocking collectives: 329 us -> none  [the longest x1 131 us: shards(): lax.all_gather(gate_weight, 'dp', axis=0, tiled=True)]
    unnamed x2 -> x0, waiting for transfers between devices: 319 us -> none
    pallas_call x0 -> x1, Pallas kernels: none -> 101 us  [module(): pl.pallas_call(functools.partial(kernel, cfg), out_shape=(jax.ShapeDtypeS...]
    psum x1 -> x0, blocking collectives: 33.6 us -> none  [shards(): branch = lax.psum(partial_out, 'mp').astype(jnp.bfloat16)]
    all_to_all x1 -> x0, starting transfers between devices: 20.4 us -> none  [shards(): lax.all_to_all(outgoing, 'dp', split_axis=0, concat_axis=0, tiled=True)]
  transfers between devices with their start and end apart: 2 -> 0, of which waited for: 1 -> 0; matrix products, arithmetic and copies ran while one was open for 1% -> 0% of each run, Pallas kernels for 0% -> 0%
where the time goes in v1:
time: 107 us
  Pallas kernels  101 us (94%)
  local copies, waits for them, and re-layouts  4.13 us (4%)
  between operations  1.3 us (1%)
    pallas_call x1, Pallas kernels, module(): pl.pallas_call(functools.partial(kernel, cfg), out_shape=(jax.ShapeDtypeS...  101 us
    unnamed x10, local copies, waits for them, and re-layouts  4.13 us

profile of v1, /device:TPU:1, one launch (start us, length us, event | category | flops | bytes accessed | tf_op | source)
XLA Modules:
  0.0 106.5 jit_solution(1652473797869549893)
XLA Ops:
  1.3 101.1 %shard_map.102 = (bf16[256,1536]{1,0:T(8,128)(2,1)}, f32[12,192]{1,0:T(8,128)}, f32[12,192]{1,0:T(8,128)}, f32[12,192]{1,0:T(8,128)}) custom-call(s32[1]{0:T(128)S(6)} %copy.15.lengths, s32[1,256]{1,0:T(1,128)} %send_order.1, bf16[256,1536]{1,0:T(8,128)(2,1)} %frames.1, bf16[12,192]{1,0:T(8,128)(2,1)} %value_w.1, bf16[12,192]{1,0:T(8,128)(2,1)} %gate_w.1, ...), custom_call_target="tpu_custom_call" | custom-call | tf_op jit(solution)/shard_map/pallas_call | solution.py:419
  102.4 0.0 copy-start.2
  102.4 2.1 %copy.16 = bf16[256,1536]{1,0:T(8,128)(2,1)} copy(bf16[256,1536]{1,0:T(8,128)(2,1)} %get-tuple-element.8) | data formatting | bytes 1572864
  104.5 0.0 copy-done.2
  104.5 0.0 copy-start.1
  104.5 0.6 copy.17
  105.1 0.1 copy-done.1
  105.2 0.0 copy-start
  105.2 0.6 copy.18
  105.8 0.1 copy-done
  105.9 0.6 copy.19
Async XLA Ops:
  102.4 2.1 %copy-start.2 = (f32[12,192]{1,0:T(8,128)S(1)}, f32[12,192]{1,0:T(8,128)}, u32[]{:S(2)}) copy-start(f32[12,192]{1,0:T(8,128)} %get-tuple-element.9) | copy-start | bytes 27652
  104.5 0.7 copy-start.1
  105.2 0.7 copy-start

commit v2 on v1

--- a/solution.py
+++ b/solution.py
@@ -61,14 +61,14 @@
 def kernel(
     cfg,
     lengths, send_order, frames, value_w, gate_w, down_w, cotangent,
-    branch, grad_value, grad_gate, grad_down,
+    branch, owned,
     out1, in1, out2, moved_parts, wide, normed,
     pack, shards, slots, weights,
-    grads, pair_out, pair_in, sums, x1_out, x1_in, x2_out, x2_in, mine, z_out, z_in, final,
+    pair_out, pair_in, sums, x1_out, x1_in, x2_out, x2_in, mine, za_out, za_in, acc, zb_out, zb_in, final,
     terms, y1_out, y1_in, y2_out, y2_in, result,
     s_w1, r_w1, s_ring, r_ring, s_sib, r_sib,
     s_a1, r_a1, s_a2, r_a2, s_ag, r_ag,
-    s_pair, r_pair, s_x, r_x, s_z, r_z, s_fin, r_fin, s_y, r_y,
+    s_pair, r_pair, s_x, r_x, s_za, r_za, s_zb, r_zb, s_fin, r_fin, s_y, r_y,
 ):
     X, Z, Y, G = cfg.X, cfg.Z, cfg.Y, cfg.G
     U = cfg.units
@@ -103,7 +103,8 @@
         partners.append(at(lax.div(t, CORES), z, lax.rem(t, CORES)))
     for o in range(1, Z):
         partners.append(at(x, mod(z + o, Z), core))
-    partners += [y_up, y_down]
+    for o in range(1, Y):
+        partners.append(at(x, z, core, mod(y + o, Y)))
     for who in partners:
         pl.semaphore_signal(barrier, inc=1, device_id=who, device_id_type=pl.DeviceIdType.MESH)
 
@@ -151,36 +152,43 @@
     ring_to = at(x, mod(z + way, Z), core)
     last = Z // 2 - 1
     half_w = cfg.zw // 2
-
-    def slot_ref(step, sign):
-        ref = slots.at[mod(z - sign * way * step, Z)]
-        return ref
-
-    def half_ref(step, part):
-        return rows_of(slots.at[mod(z - way * step, Z)], part * half_w, half_w)
-
-    ring, sib = [], []
-
-    def ring_send(step):
-        if step < last:
-            ref = slot_ref(step, 1)
-        else:
-            ref = half_ref(step, core)
-        ring.append(remote(ref, ref, s_ring.at[step], r_ring.at[step], ring_to))
-        ring[-1].start()
-
-    def ring_take(step):
-        ring[step].wait_recv()
-        if step < last:
-            ref = slot_ref(step + 1, 1)
-        else:
-            ref = half_ref(step + 1, core)
-        if step < last:
-            ring_send(step + 1)
-        sib.append(remote(ref, ref, s_sib.at[step], r_sib.at[step], sibling))
-        sib[-1].start()
-
-    ring_send(0)
+    cuts = [(lo, min(32, cfg.zw - lo)) for lo in range(0, cfg.zw, 32)]
+    half_cuts = [(lo, min(32, half_w - lo)) for lo in range(0, half_w, 32)]
+
+    ring, sib = {}, {}
+
+    def piece(hop, k):
+        ref = slots.at[mod(z - way * hop, Z)]
+        if hop <= last:
+            return rows_of(ref, *cuts[k])
+        return rows_of(ref, core * half_w + half_cuts[k][0], half_cuts[k][1])
+
+    def ring_send(hop, k):
+        ref = piece(hop, k)
+        if hop == last:
+            lo, size = half_cuts[k]
+            ref = rows_of(slots.at[mod(z - way * hop, Z)], core * half_w + lo, size)
+        ring[hop, k] = remote(ref, ref, s_ring.at[hop, k], r_ring.at[hop, k], ring_to)
+        ring[hop, k].start()
+
+    def ring_take(hop):
+        pieces = len(half_cuts) if hop == last + 1 else len(cuts)
+        for k in range(pieces):
+            ring[hop - 1, k].wait_recv()
+            if hop < last:
+                ring_send(hop, k)
+            if hop != last:
+                sib[hop, k] = remote(piece(hop, k), piece(hop, k), s_sib.at[hop - 1, k], r_sib.at[hop - 1, k], sibling)
+                sib[hop, k].start()
+        if hop == last:
+            for k in range(len(half_cuts)):
+                ring_send(hop, k)
+            for k in range(pieces):
+                sib[hop, k] = remote(piece(hop, k), piece(hop, k), s_sib.at[hop - 1, k], r_sib.at[hop - 1, k], sibling)
+                sib[hop, k].start()
+
+    for k in range(len(cuts)):
+        ring_send(0, k)
 
     for copy in a1:
         copy.wait_recv()
@@ -189,37 +197,44 @@
     g_new = lax.rem(lax.div(r_new, cfg.cap), G)
     z_new = lax.div(r_new, cfg.zrow)
     out2[...] = dot(onehot(r_old == (g_new * Z + z_new) * cfg.cap + k_new), in1[...]).astype(BF)
-    a2 = []
-    for o in range(1, Z):
+    here = moved_parts.at[y]
+    place = [0] + [2 * o - 1 if o <= Z // 2 else 2 * (Z - o) for o in range(1, Z)]
+    a2 = {}
+    for o in sorted(range(1, Z), key=lambda o: place[Z - o]):
         t = mod(z + o, Z)
-        a2.append(remote(
-            rows_of(out2, t * cfg.zrow, cfg.zrow), rows_of(moved_parts.at[y], z * cfg.zrow, cfg.zrow),
+        a2[place[Z - o]] = remote(
+            rows_of(out2, t * cfg.zrow, cfg.zrow), rows_of(here, place[Z - o] * cfg.zrow, cfg.zrow),
             s_a2.at[o], r_a2.at[o], at(x, t, core),
-        ))
-        a2[-1].start()
-    rows_of(moved_parts.at[y], z * cfg.zrow, cfg.zrow)[...] = rows_of(out2, z * cfg.zrow, cfg.zrow)[...]
-
-    for step in range(last):
-        ring_take(step)
-
-    for copy in a2:
-        copy.wait_recv()
+        )
+        a2[place[Z - o]].start()
+    here[0 : cfg.zrow, :] = rows_of(out2, z * cfg.zrow, cfg.zrow)[...]
 
     ag = []
-    for i, where in enumerate((y_up, y_down)):
-        ag.append(remote(moved_parts.at[y], moved_parts.at[y], s_ag.at[i], r_ag.at[i], where))
-        ag[-1].start()
-
-    ring_take(last)
-
-    for copy in ag[:2]:
-        copy.wait_recv()
-    for i, where in enumerate((y_up, y_down)):
-        ref = rows_of(moved_parts.at[mod(y - 1 + 2 * i, Y)], i * (R // 2), R // 2)
-        ag.append(remote(ref, ref, s_ag.at[2 + i], r_ag.at[2 + i], where))
-        ag[-1].start()
-
-    for copy in sib:
+    parcels = 4
+    each = R // parcels
+
+    def share(j):
+        for p in range(j * each // cfg.zrow, (j + 1) * each // cfg.zrow):
+            if p:
+                a2[p].wait_recv()
+        ref = rows_of(here, j * each, each)
+        for d in (1, 3, 2):
+            ag.append(remote(ref, ref, s_ag.at[j, d], r_ag.at[j, d], at(x, z, core, mod(y + d, Y))))
+            ag[-1].start()
+
+    ring_take(1)
+    ring_take(2)
+    share(0)
+    ring_take(3)
+    share(1)
+    ring_take(4)
+    share(2)
+    ring_take(5)
+    share(3)
+    for hop in range(6, last + 2):
+        ring_take(hop)
+
+    for copy in sib.values():
         copy.wait_recv()
     for xi in range(X):
         pieces = [
@@ -229,7 +244,7 @@
 
     dglu = dot(cotangent[...], weights[:, 2 * U : 3 * U])
 
-    for copy in ag[2:]:
+    for copy in ag:
         copy.wait_recv()
 
     r_new, r_old = iota((R, R), 0), iota((R, R), 1)
@@ -237,7 +252,9 @@
     c_new = lax.rem(lax.div(r_new, cfg.cap), CORES)
     z_new = lax.rem(lax.div(r_new, cfg.cap * CORES), Z)
     x_new = lax.div(r_new, cfg.cap * CORES * Z)
-    back = onehot(r_old == ((z_new * X + x_new) * CORES + c_new) * cfg.cap + k_new)
+    away = lax.rem(z_new - z + Z, Z)
+    place_new = jnp.where(away > Z // 2, 2 * (Z - away), jnp.maximum(2 * away - 1, 0))
+    back = onehot(r_old == ((place_new * X + x_new) * CORES + c_new) * cfg.cap + k_new)
     for q in range(Y):
         wide[:, q * cfg.part : (q + 1) * cfg.part] = dot(back, moved_parts[q])
     lines = 32
@@ -255,14 +272,19 @@
     d_value = (dglu * sig).astype(BF)
     d_gate = (dglu * value * sig * (1.0 - sig)).astype(BF)
 
-    grads[:, : 2 * U] = contract_rows(normed[...], jnp.concatenate([d_value, d_gate], axis=1))
-    grads[:, 2 * U :] = contract_rows(cotangent[...], glu)
+    d_both = jnp.concatenate([d_value, d_gate], axis=1)
     span = Z * cfg.pair
+    S = cfg.half
     pairs = {}
     for o in (2, 1, 3, 0):
         t = mod(x + o, X)
-        pair_out[t] = rows_of(grads, t * span + other * cfg.half, cfg.half)[...].astype(BF)
-        pairs[o] = remote(pair_out.at[t], pair_in.at[t], s_pair.at[o], r_pair.at[o], sibling)
+        cols = pl.ds(pl.multiple_of(t * span, 128), span)
+        block = jnp.concatenate(
+            [contract_rows(normed[:, cols], d_both), contract_rows(cotangent[:, cols], glu)], axis=1
+        )
+        sums[o] = jnp.where(core == 0, block[:S], block[S:])
+        pair_out[o] = jnp.where(core == 0, block[S:], block[:S]).astype(BF)
+        pairs[o] = remote(pair_out.at[o], pair_in.at[o], s_pair.at[o], r_pair.at[o], sibling)
         pairs[o].start()
 
     B = cfg.yrow
@@ -277,22 +299,33 @@
         y1[-1].start()
 
     def paired(o):
-        t = mod(x + o, X)
         pairs[o].wait_recv()
-        sums[o] = rows_of(grads, t * span + core * cfg.half, cfg.half)[...] + pair_in[t].astype(F32)
-
-    S = cfg.half
+        sums[o] = sums[o] + pair_in[o].astype(F32)
+
+    chunk = S // 2
+    part = chunk // 2
     paired(2)
     x1_out[...] = sums[2].astype(BF)
-    x1 = []
-    for i, where in enumerate((x_up, x_down)):
-        x1.append(remote(
-            x1_out.at[i * (S // 2) : (i + 1) * (S // 2)], x1_in.at[i], s_x.at[i], r_x.at[i], where,
-        ))
-        x1[-1].start()
+    x1, x2 = {}, {}
+    for q in range(2):
+        for i, where in enumerate((x_up, x_down)):
+            lo = q * chunk + i * part
+            x1[q, i] = remote(
+                x1_out.at[lo : lo + part], x1_in.at[q, i], s_x.at[q, i], r_x.at[q, i], where,
+            )
+            x1[q, i].start()
     paired(1)
     paired(3)
     paired(0)
+
+    for q in range(2):
+        for i, where in enumerate((x_up, x_down)):
+            x1[q, i].wait_recv()
+            lo = q * chunk + i * part
+            sums[1 + 2 * i, lo : lo + part, :] = sums[1 + 2 * i, lo : lo + part, :] + x1_in[q, i].astype(F32)
+            x2_out[q, i] = sums[1 + 2 * i, q * chunk : (q + 1) * chunk, :].astype(BF)
+            x2[q, i] = remote(x2_out.at[q, i], x2_in.at[q, i], s_x.at[2 + q, i], r_x.at[2 + q, i], where)
+            x2[q, i].start()
 
     y2 = []
     for i, where in enumerate((y_up, y_down)):
@@ -305,15 +338,6 @@
         y2.append(remote(y2_out.at[i], y2_in.at[i], s_y.at[2 + i], r_y.at[2 + i], where))
         y2[-1].start()
 
-    x2 = []
-    for i, where in enumerate((x_up, x_down)):
-        x1[i].wait_recv()
-        lo, hi = i * (S // 2), (i + 1) * (S // 2)
-        sums[1 + 2 * i, lo:hi, :] = sums[1 + 2 * i, lo:hi, :] + x1_in[i].astype(F32)
-        x2_out[i] = sums[1 + 2 * i].astype(BF)
-        x2.append(remote(x2_out.at[i], x2_in.at[i], s_x.at[2 + i], r_x.at[2 + i], where))
-        x2[-1].start()
-
     for copy in y2:
         copy.wait_recv()
     own_rows = (
@@ -326,17 +350,22 @@
         yg.append(remote(ref, ref, s_y.at[4 + i], r_y.at[4 + i], where))
         yg[-1].start()
 
-    for copy in x2:
-        copy.wait_recv()
-    mine[...] = sums[0] + x2_in[0].astype(F32) + x2_in[1].astype(F32)
+    for q in range(2):
+        x2[q, 0].wait_recv()
+        x2[q, 1].wait_recv()
+        lo, hi = q * chunk, (q + 1) * chunk
+        mine[lo:hi, :] = sums[0, lo:hi, :] + x2_in[q, 0].astype(F32) + x2_in[q, 1].astype(F32)
     Q = cfg.pair
-    z_out[...] = jnp.zeros_like(z_out)
-    zs = []
-    for i in range(Z // 2):
-        z_out[i, 0:Q, :] = mine[i * Q : (i + 1) * Q, :].astype(BF)
-        t = core * (Z // 2) + i
-        zs.append((t != z, remote(z_out.at[i], z_in.at[z], s_z.at[i], r_z.at[z], at(x, t, core))))
-        pl.when(t != z)(zs[-1][1].start)
+    J = Z // 2 // 4
+
+    def comb(r):
+        return [rows_of(mine, (r + 4 * j) * Q, Q, 8)[...] for j in range(J)]
+
+    za = []
+    for k, a in enumerate((1, -1, 2)):
+        za_out[k] = jnp.concatenate(comb(lax.rem(z + a + Z, 4)), axis=0).astype(BF)
+        za.append(remote(za_out.at[k], za_in.at[k], s_za.at[k], r_za.at[k], at(x, mod(z + a, Z), core)))
+        za[-1].start()
 
     for copy in yg[:2]:
         copy.wait_recv()
@@ -345,17 +374,31 @@
         yg.append(remote(ref, ref, s_y.at[6 + i], r_y.at[6 + i], where))
         yg[-1].start()
 
+    for copy in za:
+        copy.wait_recv()
+    mod4 = lax.rem(z, 4)
+    own_comb = comb(mod4)
+    arrived = za_in[0].astype(F32) + za_in[1].astype(F32) + za_in[2].astype(F32)
+    zb_out[...] = jnp.zeros_like(zb_out)
+    zb = []
+    for j in range(J):
+        part_sum = own_comb[j] + arrived[j * Q : (j + 1) * Q]
+        acc[j] = part_sum
+        zb_out[j, 0:Q, :] = part_sum.astype(BF)
+        t = core * (Z // 2) + 4 * j + mod4
+        away = lax.div(mod(z - t, Z), 4)
+        zb.append((t != z, remote(zb_out.at[j], zb_in.at[away], s_zb.at[j], r_zb.at[away], at(x, t, core))))
+        pl.when(t != z)(zb[-1][1].start)
+
     hand = remote(final, final, s_fin.at[0], r_fin.at[0], sibling)
     is_owner = lax.div(z, Z // 2) == core
 
     @pl.when(is_owner)
     def _():
-        for o in range(1, Z):
-            t = mod(z + o, Z)
-            remote(z_out.at[0], z_in.at[t], s_z.at[0], r_z.at[t], sibling).wait_recv()
-        total = rows_of(mine, (z - core * (Z // 2)) * Q, Q, 8)[...]
-        for o in range(1, Z):
-            total = total + z_in[mod(z + o, Z)][0:Q].astype(F32)
+        total = acc[lax.rem(lax.div(z, 4), J)]
+        for away in range(1, Z // 4):
+            remote(zb_out.at[0], zb_in.at[away], s_zb.at[0], r_zb.at[away], sibling).wait_recv()
+            total = total + zb_in[away, 0:Q, :].astype(F32)
         final[...] = total
         hand.start()
         hand.wait_send()
@@ -365,19 +408,26 @@
         hand.wait_recv()
 
     whole = final[...]
-    owned = jnp.where(core == 0, whole[0 : cfg.own], whole[cfg.own : 2 * cfg.own])
-    grad_value[...] = owned[:, :U]
-    grad_gate[...] = owned[:, U : 2 * U]
-    grad_down[...] = owned[:, 2 * U :]
+    owned[...] = jnp.where(core == 0, whole[0 : cfg.own], whole[cfg.own : 2 * cfg.own])
 
     for copy in yg[2:]:
         copy.wait_recv()
     branch[...] = result[...]
 
-    for copy in w1 + a1 + ring + sib + a2 + ag + list(pairs.values()) + y1 + x1 + y2 + x2 + yg:
+    for copy in w1 + a1 + ag + za + y1 + y2 + yg:
         copy.wait_send()
-    for needed, copy in zs:
+    for group in (ring, sib, a2, pairs, x1, x2):
+        for copy in group.values():
+            copy.wait_send()
+    for needed, copy in zb:
         pl.when(needed)(copy.wait_send)
+
+
+def place_results(units, branch_in, owned_in, branch, grad_value, grad_gate, grad_down):
+    branch[...] = branch_in[...]
+    grad_value[...] = owned_in[:, :units]
+    grad_gate[...] = owned_in[:, units : 2 * units]
+    grad_down[...] = owned_in[:, 2 * units :]
 
 
 def module(cfg, frames, lengths, send_order, value_weight, gate_weight, down_weight, cotangent):
@@ -396,17 +446,19 @@
         ((G * cfg.pad, C), BF),
         ((Z, cfg.zw, C), BF),
         ((D, C), BF),
-        ((D, C), F32),
         ((X, S, C), BF),
         ((X, S, C), BF),
         ((X, S, C), F32),
         ((S, C), BF),
-        ((2, S // 2, C), BF),
-        ((2, S, C), BF),
-        ((2, S, C), BF),
+        ((2, 2, S // 4, C), BF),
+        ((2, 2, S // 2, C), BF),
+        ((2, 2, S // 2, C), BF),
         ((S, C), F32),
-        ((Z // 2, cfg.pairpad, C), BF),
-        ((Z, cfg.pairpad, C), BF),
+        ((3, Z // 8 * cfg.pair, C), BF),
+        ((3, Z // 8 * cfg.pair, C), BF),
+        ((Z // 8, cfg.pair, C), F32),
+        ((Z // 8, cfg.pairpad, C), BF),
+        ((Z // 4, cfg.pairpad, C), BF),
         ((cfg.pair, C), F32),
         ((R, D), F32),
         ((B, D), BF),
@@ -415,23 +467,25 @@
         ((2, B, D), BF),
         ((R, D), BF),
     ]
-    sems = [G, Z // 2, Z // 2, G, Z, 4, X, 4, Z, 1, 8]
-    return pl.pallas_call(
+    hops = (Z // 2, -(-cfg.zw // 32))
+    sems = [(G,), hops, hops, (G,), (Z,), (4, 4), (X,), (4, 2), (3,), (Z // 4,), (1,), (8,)]
+    branch, owned = pl.pallas_call(
         functools.partial(kernel, cfg),
-        out_shape=(
-            jax.ShapeDtypeStruct((R, D), BF),
-            jax.ShapeDtypeStruct((cfg.own, U), F32),
-            jax.ShapeDtypeStruct((cfg.own, U), F32),
-            jax.ShapeDtypeStruct((cfg.own, U), F32),
-        ),
+        out_shape=(jax.ShapeDtypeStruct((R, D), BF), jax.ShapeDtypeStruct((cfg.own, C), F32)),
         in_specs=[pl.BlockSpec(memory_space=pltpu.SMEM)] + [vmem] * 6,
-        out_specs=(vmem,) * 4,
+        out_specs=(vmem,) * 2,
         scratch_shapes=[pltpu.VMEM(shape, kind) for shape, kind in buffers]
-        + [sem((n,)) for n in sems for _ in range(2)],
+        + [sem(n) for n in sems for _ in range(2)],
         compiler_params=pltpu.CompilerParams(
             collective_id=0, has_side_effects=True, vmem_limit_bytes=56 * 1024 * 1024
         ),
     )(lengths, send_order, frames, value_weight, gate_weight, down_weight, cotangent)
+    return pl.pallas_call(
+        functools.partial(place_results, U),
+        out_shape=(jax.ShapeDtypeStruct((R, D), BF),) + (jax.ShapeDtypeStruct((cfg.own, U), F32),) * 3,
+        in_specs=[vmem] * 2,
+        out_specs=(vmem,) * 4,
+    )(branch, owned)
 
 
 def build(mesh, X, Z):

time: 107 us -> 96.4 us (0.901)
  Pallas kernels: 101 us -> 95 us
  local copies, waits for them, and re-layouts: 4.13 us -> 0 us
    pallas_call x1, Pallas kernels: 101 us -> 92.9 us  [module(): pl.pallas_call(functools.partial(kernel, cfg), out_shape=(jax.ShapeDtypeS...]
    unnamed x10 -> x0, local copies, waits for them, and re-layouts: 4.13 us -> none
    pallas_call x0 -> x1, Pallas kernels: none -> 2.07 us  [module(): pl.pallas_call(functools.partial(place_results, U), out_shape=(jax.ShapeD...]
where the time goes in v2:
time: 96.4 us; the launch traced here: 96.3 us
  Pallas kernels  95 us (99%)
  between operations  1.29 us (1%)
    pallas_call x1, Pallas kernels, module(): pl.pallas_call(functools.partial(kernel, cfg), out_shape=(jax.ShapeDtypeS...  92.9 us
    pallas_call x1, Pallas kernels, module(): pl.pallas_call(functools.partial(place_results, U), out_shape=(jax.ShapeD...  2.07 us

profile of v2, /device:TPU:1, one launch (start us, length us, event | category | flops | bytes accessed | tf_op | source)
XLA Modules:
  0.0 96.3 jit_solution(12053544476030250369)
XLA Ops:
  1.3 92.9 %shard_map.102 = (bf16[256,1536]{1,0:T(8,128)(2,1)}, f32[12,576]{1,0:T(8,128)}) custom-call(s32[1]{0:T(128)S(6)} %copy.11.lengths, s32[1,256]{1,0:T(1,128)} %send_order.1, bf16[256,1536]{1,0:T(8,128)(2,1)} %frames.1, bf16[12,192]{1,0:T(8,128)(2,1)} %value_w.1, bf16[12,192]{1,0:T(8,128)(2,1)} %gate_w.1, bf16[12,192]{1,0:T(8,128)(2,1)} %down_w.1, ...), custom_call_target="tpu_custom_call" | custom-call | tf_op jit(solution)/shard_map/pallas_call | solution.py:472
  94.2 2.1 %shard_map.103 = (bf16[256,1536]{1,0:T(8,128)(2,1)}, f32[12,192]{1,0:T(8,128)}, f32[12,192]{1,0:T(8,128)}, f32[12,192]{1,0:T(8,128)}) custom-call(bf16[256,1536]{1,0:T(8,128)(2,1)} %get-tuple-element.6.branch_in, f32[12,576]{1,0:T(8,128)} %get-tuple-element.7.owned_in), custom_call_target="tpu_custom_call" | custom-call | tf_op jit(solution)/shard_map/pallas_call | solution.py:483

commit v3 on v0

v3 whole, which is shorter than its diff:
```python
import functools

import jax
import jax.numpy as jnp
from jax import lax
from jax.experimental import pallas as pl
from jax.experimental.pallas import tpu as pltpu
from jax.sharding import PartitionSpec as P

CORES = 2
BF = jnp.bfloat16
F32 = jnp.float32


def ceil16(rows):
    return -(-rows // 16) * 16


def iota(shape, axis):
    return lax.broadcasted_iota(jnp.int32, shape, axis)


def onehot(hit):
    return jnp.where(hit, 1.0, 0.0).astype(BF)


def dot(left, right):
    return jnp.dot(left, right, preferred_element_type=F32)


def contract_rows(left, right):
    return lax.dot_general(left, right, (((0,), (0,)), ((), ())), preferred_element_type=F32)


def contract_cols(left, right):
    return lax.dot_general(left, right, (((1,), (1,)), ((), ())), preferred_element_type=F32)


def mod(value, count):
    return lax.rem(value + count, count)


class Sizes:
    def __init__(self, X, Z, Y, rows, width, own, units):
        self.X, self.Z, self.Y = X, Z, Y
        self.G = X * CORES
        self.rows, self.width, self.own, self.units = rows, width, own, units
        self.cap = rows // (X * Z * CORES)
        self.part = width // Y
        self.pad = ceil16(own)
        self.zrow = self.G * self.cap
        self.grow = self.Z * self.cap
        self.far = Z // 4
        self.comb = self.far * own
        self.pair = CORES * own
        self.pairpad = ceil16(self.pair)
        self.cols = 3 * units
        self.half = Z // 2 * self.pair
        self.yrow = rows // Y


def kernel(
    cfg,
    lengths, send_order, frames, value_w, gate_w, down_w, cotangent,
    branch, owned,
    out1, in1, out2, moved, normed, cot, glu_rows,
    shards, w_own, w_sib, weights,
    block, pair_out, pair_in, x_out, x_in, near_out, near_in, acc, far_out, far_in, final,
    y_own, y_out, y_in, result,
    s_a1, r_a1, s_a2, r_a2, s_ag, r_ag,
    s_wf, r_wf, s_wn, r_wn, s_wx, r_wx, s_sib, r_sib,
    s_pair, r_pair, s_x, r_x, s_near, r_near, s_far, r_far, s_fin, r_fin, s_y, r_y, s_yg, r_yg,
    relay,
):
    X, Z, Y, G = cfg.X, cfg.Z, cfg.Y, cfg.G
    R, U, F, cap = cfg.rows, cfg.units, cfg.far, cfg.cap
    dp = lax.axis_index("dp")
    y = lax.axis_index("mp")
    core = lax.rem(dp, CORES)
    z = lax.rem(lax.div(dp, CORES), Z)
    x = lax.div(dp, CORES * Z)
    g = x * CORES + core
    other = 1 - core
    sibling = {"dp": dp + 1 - 2 * core, "mp": y}

    def at(x_, z_, core_):
        return {"dp": (x_ * Z + z_) * CORES + core_, "mp": y}

    def at_x(o):
        return at(mod(x + o, X), z, core)

    def at_z(o):
        return at(x, mod(z + o, Z), core)

    def at_y(o):
        return {"dp": dp, "mp": mod(y + o, Y)}

    def at_g(t):
        return at(lax.div(t, CORES), z, lax.rem(t, CORES))

    def send(src, dst, sent, arrived, where):
        copy = pltpu.make_async_remote_copy(
            src_ref=src, dst_ref=dst, send_sem=sent, recv_sem=arrived,
            device_id=where, device_id_type=pl.DeviceIdType.MESH,
        )
        copy.start()

    def drain(sem, ref):
        pltpu.make_async_copy(ref, ref, sem).wait()

    def rows_of(ref, start, size, step=16):
        return ref.at[pl.ds(pl.multiple_of(start, step), size)]

    barrier = pltpu.get_barrier_semaphore()
    partners = [at_g(mod(g + o, G)) for o in range(1, G)]
    partners += [at_z(o * s) for o in range(1, 5) for s in (1, -1)]
    partners += [at_y(o) for o in range(1, Y)]
    for who in partners:
        pl.semaphore_signal(barrier, inc=1, device_id=who, device_id_type=pl.DeviceIdType.MESH)

    packed = jnp.concatenate([value_w[...], gate_w[...], down_w[...]], axis=1)
    mine = shards.at[1, 0 : cfg.pad]
    mine[...] = jnp.zeros_like(mine)
    shards[1, 0 : cfg.own, :] = packed

    row, place = iota((R, R), 0), iota((1, R), 1)
    k_of, z_of, g_of = lax.rem(place, cap), lax.rem(lax.div(place, cap), Z), lax.div(place, cap * Z)
    natural = ((lax.div(g_of, CORES) * Z + z_of) * CORES + lax.rem(g_of, CORES)) * cap + k_of
    numbers = jnp.broadcast_to(send_order[...].astype(F32).astype(BF), (16, R))
    order = dot(numbers, onehot(row == natural))[0:1, :]
    pick = onehot((row.astype(F32) == order) & (row < lengths[0]))
    columns = pl.ds(pl.multiple_of(y * cfg.part, 128), cfg.part)
    out1[...] = contract_rows(pick, frames[:, columns]).astype(BF)

    pl.semaphore_wait(barrier, len(partners))
    for o in (4, -4):
        pl.semaphore_signal(relay, inc=1, device_id=at_z(o), device_id_type=pl.DeviceIdType.MESH)

    for o in range(1, G):
        t = mod(g + o, G)
        send(
            rows_of(out1, t * cfg.grow, cfg.grow), rows_of(in1, g * cfg.grow, cfg.grow),
            s_a1, r_a1, at_g(t),
        )
    rows_of(in1, g * cfg.grow, cfg.grow)[...] = rows_of(out1, g * cfg.grow, cfg.grow)[...]

    def far_shard(f):
        send(mine, shards.at[1, f * cfg.pad : (f + 1) * cfg.pad], s_wf, r_wf, at_z(4 * f))

    for f in range(1, F):
        if 4 * f != Z // 2:
            far_shard(f)
    near = (1, -1, 2)
    for a in near:
        send(mine, shards.at[a + 1, 0 : cfg.pad], s_wn, r_wn.at[a + 1], at_z(a))

    to_new = (z_of * G + g_of) * cap + k_of
    drain(r_a1, in1.at[0 : (G - 1) * cfg.grow])
    out2[...] = dot(onehot(row == to_new), in1[...]).astype(BF)
    here = moved.at[y]
    position = [0] + [2 * o - 1 if o <= Z // 2 else 2 * (Z - o) for o in range(1, Z)]
    parcels = 4
    each = R // parcels
    per = each // cfg.zrow
    pl.semaphore_wait(relay, 2)
    for o in sorted(range(1, Z), key=lambda o: position[Z - o]):
        p = position[Z - o]
        send(
            rows_of(out2, mod(z + o, Z) * cfg.zrow, cfg.zrow), here.at[p * cfg.zrow : (p + 1) * cfg.zrow],
            s_a2, r_a2.at[p // per], at_z(o),
        )
    far_shard(F // 2)
    here[0 : cfg.zrow, :] = rows_of(out2, z * cfg.zrow, cfg.zrow)[...]

    q = iota((1, F * cfg.pad), 1)
    j = lax.rem(q, cfg.pad)
    squeeze = onehot(
        iota((cfg.comb, F * cfg.pad), 0) == jnp.where(j < cfg.own, lax.div(q, cfg.pad) * cfg.own + j, -1)
    )

    def spread(n):
        w_own[n, 0] = dot(squeeze, shards[n]).astype(BF)
        for k in (2, 1, 3):
            send(w_own.at[n, 0], w_own.at[n, k], s_wx, r_wx.at[n], at_x(k))
        send(w_own.at[n, 0], w_sib.at[n, 0], s_sib.at[0], r_sib.at[0], sibling)

    def hand_on(n):
        drain(r_wx.at[n], w_own.at[n, 1:X])
        send(w_own.at[n, 1:X], w_sib.at[n, 1:X], s_sib.at[1], r_sib.at[1], sibling)

    drain(r_wf, shards.at[1, cfg.pad :])
    for a in near:
        send(shards.at[1, cfg.pad :], shards.at[a + 1, cfg.pad :], s_wn, r_wn.at[a + 1], at_z(a))
    spread(1)

    where = lax.div(place, cfg.zrow)
    away = jnp.where(lax.rem(where, 2) == 1, lax.div(where + 1, 2), lax.rem(Z - lax.div(where, 2), Z))
    k_at, g_at = lax.rem(place, cap), lax.rem(lax.div(place, cap), G)
    natural = (
        (lax.div(g_at, CORES) * Z + lax.rem(z + away, Z)) * CORES + lax.rem(g_at, CORES)
    ) * cap + k_at
    back = onehot(row == natural)
    cot[...] = contract_rows(back, cotangent[...]).astype(BF)

    def share(j):
        drain(r_a2.at[j], here.at[(0 if j else cfg.zrow) : each])
        ref = here.at[j * each : (j + 1) * each]
        for d in (2, 1, 3):
            send(ref, ref, s_ag, r_ag.at[j], at_y(d))

    def normalize(j):
        drain(r_ag.at[j], moved.at[0, 0 : (Y - 1) * each])
        lines = 32
        for i in range(each // lines):
            span = slice(j * each + i * lines, j * each + (i + 1) * lines)
            parts = [moved[c, span, :].astype(F32) for c in range(Y)]
            mean = sum(jnp.sum(p, axis=1, keepdims=True) for p in parts) / cfg.width
            parts = [p - mean for p in parts]
            var = sum(jnp.sum(jnp.square(p), axis=1, keepdims=True) for p in parts) / cfg.width
            scale = lax.rsqrt(var + 1e-05)
            for c in range(Y):
                normed[span, c * cfg.part : (c + 1) * cfg.part] = (parts[c] * scale).astype(BF)

    share(0)
    for a in near:
        drain(r_wn.at[a + 1], shards.at[a + 1])
        spread(a + 1)
    share(1)
    hand_on(1)
    share(2)
    for a in near:
        hand_on(a + 1)
    normalize(0)
    share(3)
    normalize(1)

    q = iota((1, 2 * 4 * cfg.comb), 1)
    side = lax.div(q, 4 * cfg.comb)
    n_of = lax.rem(lax.div(q, cfg.comb), 4)
    f_of = lax.rem(lax.div(q, cfg.own), F)
    z_of = lax.rem(z - (n_of - 1) - 4 * f_of + 2 * Z, Z)
    core_of = core + side - 2 * core * side
    natural = (z_of * CORES + core_of) * cfg.own + lax.rem(q, cfg.own)
    span = Z * cfg.pair
    spot = onehot(iota((span, span), 0) == natural)
    drain(r_sib.at[0], w_sib.at[:, 0])
    drain(r_sib.at[1], w_sib.at[:, 1:X])
    for k in range(X):
        pieces = [w[n, k] for w in (w_own, w_sib) for n in range(4)]
        rows_of(weights, mod(x - k, X) * span, span)[...] = dot(
            spot, jnp.concatenate(pieces, axis=0)
        ).astype(BF)

    dglu = dot(cot[...], weights[:, 2 * U : 3 * U])
    normalize(2)
    normalize(3)

    both = dot(normed[...], weights[:, : 2 * U])
    value, gate = both[:, :U], both[:, U : 2 * U]
    sig = jax.nn.sigmoid(gate)
    glu = (value * sig).astype(BF)
    d_value = (dglu * sig).astype(BF)
    d_gate = (dglu * value * sig * (1.0 - sig)).astype(BF)

    d_both = jnp.concatenate([d_value, d_gate], axis=1)
    J = Z // 2 // 4
    steps = (2, 1, -1, 0)
    Q = cfg.pair

    def chunk(o, half, a):
        r = lax.rem(z + a + Z, 4)
        return jnp.concatenate(
            [rows_of(block.at[o], (half * (Z // 2) + r + 4 * j) * Q, Q, 8)[...] for j in range(J)], axis=0
        )

    for o in (2, 1, 3, 0):
        cols = pl.ds(pl.multiple_of(mod(x + o, X) * span, 128), span)
        block[o] = jnp.concatenate(
            [contract_rows(normed[:, cols], d_both), contract_rows(cot[:, cols], glu)], axis=1
        )
        for i, a in enumerate(steps):
            pair_out[o, i] = chunk(o, other, a).astype(BF)
        send(pair_out.at[o], pair_in.at[o], s_pair, r_pair.at[o], sibling)

    glu_rows[...] = dot(back, glu).astype(BF)
    B = cfg.yrow
    for d in (2, 1, 3):
        mine_y = rows_of(glu_rows, mod(y + d, Y) * B, B)
        y_out[d - 1] = contract_cols(mine_y[...], weights[:, 2 * U : 3 * U]).astype(BF)
        send(y_out.at[d - 1], y_in.at[d - 1], s_y, r_y, at_y(d))
    y_own[...] = contract_cols(rows_of(glu_rows, y * B, B)[...], weights[:, 2 * U : 3 * U])

    for o in (2, 1, 3):
        drain(r_pair.at[o], pair_in.at[o])
    for i, a in enumerate(steps):
        for o in (2, 1, 3):
            x_out[i, o - 1] = (chunk(o, core, a) + pair_in[o, i].astype(F32)).astype(BF)
            send(x_out.at[i, o - 1], x_in.at[i, o - 1], s_x, r_x.at[i], at_x(o))
    drain(r_pair.at[0], pair_in.at[0])

    def summed(i, a):
        drain(r_x.at[i], x_in.at[i])
        total = chunk(0, core, a) + pair_in[0, i].astype(F32)
        for k in range(X - 1):
            total = total + x_in[i, k].astype(F32)
        return total

    def to_near(i):
        near_out[i] = summed(i, steps[i]).astype(BF)
        send(near_out.at[i], near_in.at[i], s_near, r_near, at_z(steps[i]))

    to_near(0)

    drain(r_y, y_in)
    rows_of(result, y * B, B)[...] = (
        y_own[...] + y_in[0].astype(F32) + y_in[1].astype(F32) + y_in[2].astype(F32)
    ).astype(BF)
    for d in (2, 1, 3):
        send(rows_of(result, y * B, B), rows_of(result, y * B, B), s_yg, r_yg, at_y(d))

    to_near(1)
    to_near(2)
    total = summed(3, 0)
    drain(r_near, near_in)
    for i in range(3):
        total = total + near_in[i].astype(F32)

    far_out[...] = jnp.zeros_like(far_out)
    sends = []
    for j in range(J):
        part = total[j * Q : (j + 1) * Q]
        acc[j] = part
        far_out[j, 0:Q, :] = part.astype(BF)
        t = core * (Z // 2) + 4 * j + lax.rem(z, 4)
        slot = lax.div(mod(z - t, Z), 4)
        copy = pltpu.make_async_remote_copy(
            src_ref=far_out.at[j], dst_ref=far_in.at[slot], send_sem=s_far.at[j], recv_sem=r_far,
            device_id=at(x, t, core), device_id_type=pl.DeviceIdType.MESH,
        )
        sends.append((t != z, copy))
        pl.when(t != z)(copy.start)

    is_owner = lax.div(z, Z // 2) == core
    hand = pltpu.make_async_remote_copy(
        src_ref=final, dst_ref=final, send_sem=s_fin, recv_sem=r_fin,
        device_id=sibling, device_id_type=pl.DeviceIdType.MESH,
    )

    @pl.when(is_owner)
    def _():
        whole = acc[lax.rem(lax.div(z, 4), J)]
        drain(r_far, far_in.at[1:F])
        for slot in range(1, F):
            whole = whole + far_in[slot, 0:Q, :].astype(F32)
        final[...] = whole
        hand.start()
        hand.wait_send()

    @pl.when(jnp.logical_not(is_owner))
    def _():
        hand.wait_recv()

    whole = final[...]
    owned[...] = jnp.where(core == 0, whole[0 : cfg.own], whole[cfg.own : 2 * cfg.own])

    drain(r_yg, result.at[0 : (Y - 1) * B])
    branch[...] = result[...]

    drain(s_a1, out1.at[0 : (G - 1) * cfg.grow])
    drain(s_a2, out2.at[0 : (Z - 1) * cfg.zrow])
    drain(s_ag, moved.at[0 : Y - 1])
    drain(s_wf, shards.at[1, cfg.pad :])
    drain(s_wn, shards.at[0:3])
    drain(s_wx, w_own.at[:, 1:X])
    drain(s_sib.at[0], w_sib.at[:, 0])
    drain(s_sib.at[1], w_sib.at[:, 1:X])
    drain(s_pair, pair_out)
    drain(s_x, x_out)
    drain(s_near, near_out)
    drain(s_y, y_out)
    drain(s_yg, result.at[0 : (Y - 1) * B])
    for needed, copy in sends:
        pl.when(needed)(copy.wait_send)


def place_results(units, branch_in, owned_in, branch, grad_value, grad_gate, grad_down):
    branch[...] = branch_in[...]
    grad_value[...] = owned_in[:, :units]
    grad_gate[...] = owned_in[:, units : 2 * units]
    grad_down[...] = owned_in[:, 2 * units :]


def module(cfg, frames, lengths, send_order, value_weight, gate_weight, down_weight, cotangent):
    X, Z, Y, G, R, D, U = cfg.X, cfg.Z, cfg.Y, cfg.G, cfg.rows, cfg.width, cfg.units
    C, S, B = cfg.cols, cfg.half, cfg.yrow
    vmem = pl.BlockSpec(memory_space=pltpu.VMEM)
    sem = pltpu.SemaphoreType.DMA
    F, J, H = cfg.far, Z // 8, Z // 8 * cfg.pair
    buffers = [
        ((R, cfg.part), BF),
        ((R, cfg.part), BF),
        ((R, cfg.part), BF),
        ((Y, R, cfg.part), BF),
        ((R, D), BF),
        ((R, D), BF),
        ((R, U), BF),
        ((4, F * cfg.pad, C), BF),
        ((4, X, cfg.comb, C), BF),
        ((4, X, cfg.comb, C), BF),
        ((D, C), BF),
        ((X, Z * cfg.pair, C), F32),
        ((X, 4, H, C), BF),
        ((X, 4, H, C), BF),
        ((4, X - 1, H, C), BF),
        ((4, X - 1, H, C), BF),
        ((3, H, C), BF),
        ((3, H, C), BF),
        ((J, cfg.pair, C), F32),
        ((J, cfg.pairpad, C), BF),
        ((F, cfg.pairpad, C), BF),
        ((cfg.pair, C), F32),
        ((B, D), F32),
        ((Y - 1, B, D), BF),
        ((Y - 1, B, D), BF),
        ((R, D), BF),
    ]
    one = ()
    sems = [
        one, one, one, (4,), one, (4,),
        one, one, one, (4,), one, (4,), (2,), (2,),
        one, (X,), one, (4,), one, one, (J,), one, one, one,
        one, one, one, one,
    ]
    branch, owned = pl.pallas_call(
        functools.partial(kernel, cfg),
        out_shape=(jax.ShapeDtypeStruct((R, D), BF), jax.ShapeDtypeStruct((cfg.own, C), F32)),
        in_specs=[pl.BlockSpec(memory_space=pltpu.SMEM)] + [vmem] * 6,
        out_specs=(vmem,) * 2,
        scratch_shapes=[pltpu.VMEM(shape, kind) for shape, kind in buffers]
        + [sem(n) for n in sems]
        + [pltpu.SemaphoreType.REGULAR],
        compiler_params=pltpu.CompilerParams(
            collective_id=0, has_side_effects=True, vmem_limit_bytes=56 * 1024 * 1024
        ),
    )(lengths, send_order, frames, value_weight, gate_weight, down_weight, cotangent)
    return pl.pallas_call(
        functools.partial(place_results, U),
        out_shape=(jax.ShapeDtypeStruct((R, D), BF),) + (jax.ShapeDtypeStruct((cfg.own, U), F32),) * 3,
        in_specs=[vmem] * 2,
        out_specs=(vmem,) * 4,
    )(branch, owned)


def build(mesh, X, Z):
    def shards(frames, lengths, send_order, value_weight, gate_weight, down_weight, cotangent):
        cfg = Sizes(
            X, Z, mesh.shape["mp"], frames.shape[0], frames.shape[1],
            value_weight.shape[0], value_weight.shape[1],
        )
        return module(
            cfg, frames, lengths, send_order, value_weight, gate_weight, down_weight, cotangent
        )

    return jax.shard_map(
        shards,
        mesh=mesh,
        in_specs=(
            P("dp", None),
            P("dp"),
            P("dp", None),
            P("dp", "mp"),
            P("dp", "mp"),
            P("dp", "mp"),
            P("dp", None),
        ),
        out_specs=(P("dp", None), P("dp", "mp"), P("dp", "mp"), P("dp", "mp")),
        check_vma=False,
    )


def solution(mesh):
    return build(mesh, 4, 16)
```

time: 745 us -> 86.8 us (0.12)
  blocking collectives: 363 us -> 0 us
  waiting for transfers between devices: 319 us -> 0 us
  Pallas kernels: 0 us -> 85.3 us
  starting transfers between devices: 20.4 us -> 0 us
  between operations: 15.6 us -> 1.29 us
  local copies, waits for them, and re-layouts: 12.2 us -> 0 us
  other arithmetic: 9.98 us -> 0 us
    all_gather x3 -> x0, blocking collectives: 329 us -> none  [the longest x1 131 us: shards(): lax.all_gather(gate_weight, 'dp', axis=0, tiled=True)]
    unnamed x2 -> x0, waiting for transfers between devices: 319 us -> none
    pallas_call x0 -> x2, Pallas kernels: none -> 85.3 us  [the longest x1 83.2 us: module(): pl.pallas_call(functools.partial(kernel, cfg), out_shape=(jax.ShapeDtypeS...]
    psum x1 -> x0, blocking collectives: 33.6 us -> none  [shards(): branch = lax.psum(partial_out, 'mp').astype(jnp.bfloat16)]
    all_to_all x1 -> x0, starting transfers between devices: 20.4 us -> none  [shards(): lax.all_to_all(outgoing, 'dp', split_axis=0, concat_axis=0, tiled=True)]
    unnamed x22 -> x0, local copies, waits for them, and re-layouts: 7.59 us -> none
  transfers between devices with their start and end apart: 2 -> 0, of which waited for: 1 -> 0; matrix products, arithmetic and copies ran while one was open for 1% -> 0% of each run, Pallas kernels for 0% -> 0%
where the time goes in v3:
time: 86.8 us; the launch traced here: 86.6 us
  Pallas kernels  85.3 us (98%)
  between operations  1.29 us (1%)
    pallas_call x1, Pallas kernels, module(): pl.pallas_call(functools.partial(kernel, cfg), out_shape=(jax.ShapeDtypeS...  83.2 us
    pallas_call x1, Pallas kernels, module(): pl.pallas_call(functools.partial(place_results, U), out_shape=(jax.ShapeD...  2.07 us

profile of v3, /device:TPU:1, one launch (start us, length us, event | category | flops | bytes accessed | tf_op | source)
XLA Modules:
  0.0 86.6 jit_solution(5914758986434193600)
XLA Ops:
  1.3 83.2 %shard_map.102 = (bf16[256,1536]{1,0:T(8,128)(2,1)}, f32[12,576]{1,0:T(8,128)}) custom-call(s32[1]{0:T(128)S(6)} %copy.11.lengths, s32[1,256]{1,0:T(1,128)} %send_order.1, bf16[256,1536]{1,0:T(8,128)(2,1)} %frames.1, bf16[12,192]{1,0:T(8,128)(2,1)} %value_w.1, bf16[12,192]{1,0:T(8,128)(2,1)} %gate_w.1, bf16[12,192]{1,0:T(8,128)(2,1)} %down_w.1, ...), custom_call_target="tpu_custom_call" | custom-call | tf_op jit(solution)/shard_map/pallas_call | solution.py:434
  84.5 2.1 %shard_map.103 = (bf16[256,1536]{1,0:T(8,128)(2,1)}, f32[12,192]{1,0:T(8,128)}, f32[12,192]{1,0:T(8,128)}, f32[12,192]{1,0:T(8,128)}) custom-call(bf16[256,1536]{1,0:T(8,128)(2,1)} %get-tuple-element.6.branch_in, f32[12,576]{1,0:T(8,128)} %get-tuple-element.7.owned_in), custom_call_target="tpu_custom_call" | custom-call | tf_op jit(solution)/shard_map/pallas_call | solution.py:446

commit v4 on v3

--- a/solution.py
+++ b/solution.py
@@ -51,7 +51,7 @@
         self.zrow = self.G * self.cap
         self.grow = self.Z * self.cap
         self.far = Z // 4
-        self.comb = self.far * own
+        self.comb = 4 * own
         self.pair = CORES * own
         self.pairpad = ceil16(self.pair)
         self.cols = 3 * units
@@ -119,9 +119,9 @@
         pl.semaphore_signal(barrier, inc=1, device_id=who, device_id_type=pl.DeviceIdType.MESH)
 
     packed = jnp.concatenate([value_w[...], gate_w[...], down_w[...]], axis=1)
-    mine = shards.at[1, 0 : cfg.pad]
+    mine = shards.at[0, cfg.pad : 2 * cfg.pad]
     mine[...] = jnp.zeros_like(mine)
-    shards[1, 0 : cfg.own, :] = packed
+    shards[0, cfg.pad : cfg.pad + cfg.own, :] = packed
 
     row, place = iota((R, R), 0), iota((1, R), 1)
     k_of, z_of, g_of = lax.rem(place, cap), lax.rem(lax.div(place, cap), Z), lax.div(place, cap * Z)
@@ -144,15 +144,23 @@
         )
     rows_of(in1, g * cfg.grow, cfg.grow)[...] = rows_of(out1, g * cfg.grow, cfg.grow)[...]
 
-    def far_shard(f):
-        send(mine, shards.at[1, f * cfg.pad : (f + 1) * cfg.pad], s_wf, r_wf, at_z(4 * f))
-
+    near = (1, -1, 2)
+
+    def pass_near(f):
+        ref = shards.at[f, cfg.pad : 2 * cfg.pad]
+        for a in near:
+            lo = (a + 1) * cfg.pad
+            send(ref, shards.at[f, lo : lo + cfg.pad], s_wn, r_wn.at[f], at_z(a))
+
+    def pass_far(f):
+        send(mine, shards.at[f, cfg.pad : 2 * cfg.pad], s_wf, r_wf.at[f], at_z(4 * f))
+
+    pass_near(0)
     for f in range(1, F):
         if 4 * f != Z // 2:
-            far_shard(f)
-    near = (1, -1, 2)
-    for a in near:
-        send(mine, shards.at[a + 1, 0 : cfg.pad], s_wn, r_wn.at[a + 1], at_z(a))
+            pass_far(f)
+    pl.semaphore_wait(relay, 2)
+    pass_far(F // 2)
 
     to_new = (z_of * G + g_of) * cap + k_of
     drain(r_a1, in1.at[0 : (G - 1) * cfg.grow])
@@ -162,36 +170,41 @@
     parcels = 4
     each = R // parcels
     per = each // cfg.zrow
-    pl.semaphore_wait(relay, 2)
-    for o in sorted(range(1, Z), key=lambda o: position[Z - o]):
-        p = position[Z - o]
-        send(
-            rows_of(out2, mod(z + o, Z) * cfg.zrow, cfg.zrow), here.at[p * cfg.zrow : (p + 1) * cfg.zrow],
-            s_a2, r_a2.at[p // per], at_z(o),
-        )
-    far_shard(F // 2)
+    def to_z(parcel_range):
+        for o in sorted(range(1, Z), key=lambda o: position[Z - o]):
+            p = position[Z - o]
+            if p // per in parcel_range:
+                send(
+                    rows_of(out2, mod(z + o, Z) * cfg.zrow, cfg.zrow),
+                    here.at[p * cfg.zrow : (p + 1) * cfg.zrow],
+                    s_a2, r_a2.at[p // per], at_z(o),
+                )
+
+    to_z((0, 1))
     here[0 : cfg.zrow, :] = rows_of(out2, z * cfg.zrow, cfg.zrow)[...]
 
-    q = iota((1, F * cfg.pad), 1)
+    q = iota((1, 4 * cfg.pad), 1)
     j = lax.rem(q, cfg.pad)
     squeeze = onehot(
-        iota((cfg.comb, F * cfg.pad), 0) == jnp.where(j < cfg.own, lax.div(q, cfg.pad) * cfg.own + j, -1)
+        iota((cfg.comb, 4 * cfg.pad), 0) == jnp.where(j < cfg.own, lax.div(q, cfg.pad) * cfg.own + j, -1)
     )
 
-    def spread(n):
-        w_own[n, 0] = dot(squeeze, shards[n]).astype(BF)
+    def spread(f):
+        drain(r_wn.at[f], shards.at[f, 0 : 3 * cfg.pad])
+        w_own[f, 0] = dot(squeeze, shards[f]).astype(BF)
         for k in (2, 1, 3):
-            send(w_own.at[n, 0], w_own.at[n, k], s_wx, r_wx.at[n], at_x(k))
-        send(w_own.at[n, 0], w_sib.at[n, 0], s_sib.at[0], r_sib.at[0], sibling)
-
-    def hand_on(n):
-        drain(r_wx.at[n], w_own.at[n, 1:X])
-        send(w_own.at[n, 1:X], w_sib.at[n, 1:X], s_sib.at[1], r_sib.at[1], sibling)
-
-    drain(r_wf, shards.at[1, cfg.pad :])
-    for a in near:
-        send(shards.at[1, cfg.pad :], shards.at[a + 1, cfg.pad :], s_wn, r_wn.at[a + 1], at_z(a))
-    spread(1)
+            send(w_own.at[f, 0], w_own.at[f, k], s_wx, r_wx.at[f], at_x(k))
+
+    def hand_on(f):
+        drain(r_wx.at[f], w_own.at[f, 1:X])
+        send(w_own.at[f], w_sib.at[f], s_sib, r_sib, sibling)
+
+    spread(0)
+    for f in (1, 3, 2):
+        if f < F:
+            drain(r_wf.at[f], shards.at[f, cfg.pad : 2 * cfg.pad])
+            pass_near(f)
+    to_z((2, 3))
 
     where = lax.div(place, cfg.zrow)
     away = jnp.where(lax.rem(where, 2) == 1, lax.div(where + 1, 2), lax.rem(Z - lax.div(where, 2), Z))
@@ -222,37 +235,39 @@
                 normed[span, c * cfg.part : (c + 1) * cfg.part] = (parts[c] * scale).astype(BF)
 
     share(0)
-    for a in near:
-        drain(r_wn.at[a + 1], shards.at[a + 1])
-        spread(a + 1)
-    share(1)
+    for f in (1, 3, 2):
+        if f < F:
+            spread(f)
+        if f == 3:
+            share(1)
+    hand_on(0)
+    share(2)
     hand_on(1)
-    share(2)
-    for a in near:
-        hand_on(a + 1)
     normalize(0)
     share(3)
+    for f in (3, 2):
+        if f < F:
+            hand_on(f)
     normalize(1)
-
-    q = iota((1, 2 * 4 * cfg.comb), 1)
-    side = lax.div(q, 4 * cfg.comb)
-    n_of = lax.rem(lax.div(q, cfg.comb), 4)
-    f_of = lax.rem(lax.div(q, cfg.own), F)
+    normalize(2)
+
+    q = iota((1, 2 * F * cfg.comb), 1)
+    side = lax.div(q, F * cfg.comb)
+    f_of = lax.rem(lax.div(q, cfg.comb), F)
+    n_of = lax.rem(lax.div(q, cfg.own), 4)
     z_of = lax.rem(z - (n_of - 1) - 4 * f_of + 2 * Z, Z)
     core_of = core + side - 2 * core * side
     natural = (z_of * CORES + core_of) * cfg.own + lax.rem(q, cfg.own)
     span = Z * cfg.pair
     spot = onehot(iota((span, span), 0) == natural)
-    drain(r_sib.at[0], w_sib.at[:, 0])
-    drain(r_sib.at[1], w_sib.at[:, 1:X])
+    drain(r_sib, w_sib)
     for k in range(X):
-        pieces = [w[n, k] for w in (w_own, w_sib) for n in range(4)]
+        pieces = [w[f, k] for w in (w_own, w_sib) for f in range(F)]
         rows_of(weights, mod(x - k, X) * span, span)[...] = dot(
             spot, jnp.concatenate(pieces, axis=0)
         ).astype(BF)
 
     dglu = dot(cot[...], weights[:, 2 * U : 3 * U])
-    normalize(2)
     normalize(3)
 
     both = dot(normed[...], weights[:, : 2 * U])
@@ -369,11 +384,10 @@
     drain(s_a1, out1.at[0 : (G - 1) * cfg.grow])
     drain(s_a2, out2.at[0 : (Z - 1) * cfg.zrow])
     drain(s_ag, moved.at[0 : Y - 1])
-    drain(s_wf, shards.at[1, cfg.pad :])
-    drain(s_wn, shards.at[0:3])
+    drain(s_wf, shards.at[0, 0 : (F - 1) * cfg.pad])
+    drain(s_wn, shards.at[:, 0 : 3 * cfg.pad])
     drain(s_wx, w_own.at[:, 1:X])
-    drain(s_sib.at[0], w_sib.at[:, 0])
-    drain(s_sib.at[1], w_sib.at[:, 1:X])
+    drain(s_sib, w_own)
     drain(s_pair, pair_out)
     drain(s_x, x_out)
     drain(s_near, near_out)
@@ -404,9 +418,9 @@
         ((R, D), BF),
         ((R, D), BF),
         ((R, U), BF),
-        ((4, F * cfg.pad, C), BF),
-        ((4, X, cfg.comb, C), BF),
-        ((4, X, cfg.comb, C), BF),
+        ((F, 4 * cfg.pad, C), BF),
+        ((F, X, cfg.comb, C), BF),
+        ((F, X, cfg.comb, C), BF),
         ((D, C), BF),
         ((X, Z * cfg.pair, C), F32),
         ((X, 4, H, C), BF),
@@ -427,7 +441,7 @@
     one = ()
     sems = [
         one, one, one, (4,), one, (4,),
-        one, one, one, (4,), one, (4,), (2,), (2,),
+        one, (F,), one, (F,), one, (F,), one, one,
         one, (X,), one, (4,), one, one, (J,), one, one, one,
         one, one, one, one,
     ]

time: 86.8 us -> 75.4 us (0.87)
  Pallas kernels: 85.3 us -> 73.9 us
    pallas_call x1, Pallas kernels: 83.2 us -> 71.9 us  [module(): pl.pallas_call(functools.partial(kernel, cfg), out_shape=(jax.ShapeDtypeS...]
where the time goes in v4:
time: 75.4 us; the launch traced here: 75.2 us
  Pallas kernels  73.9 us (98%)
  between operations  1.29 us (2%)
    pallas_call x1, Pallas kernels, module(): pl.pallas_call(functools.partial(kernel, cfg), out_shape=(jax.ShapeDtypeS...  71.9 us
    pallas_call x1, Pallas kernels, module(): pl.pallas_call(functools.partial(place_results, U), out_shape=(jax.ShapeD...  2.07 us

profile of v4, /device:TPU:1, one launch (start us, length us, event | category | flops | bytes accessed | tf_op | source)
XLA Modules:
  0.0 75.2 jit_solution(5046155759950352787)
XLA Ops:
  1.3 71.9 %shard_map.102 = (bf16[256,1536]{1,0:T(8,128)(2,1)}, f32[12,576]{1,0:T(8,128)}) custom-call(s32[1]{0:T(128)S(6)} %copy.11.lengths, s32[1,256]{1,0:T(1,128)} %send_order.1, bf16[256,1536]{1,0:T(8,128)(2,1)} %frames.1, bf16[12,192]{1,0:T(8,128)(2,1)} %value_w.1, bf16[12,192]{1,0:T(8,128)(2,1)} %gate_w.1, bf16[12,192]{1,0:T(8,128)(2,1)} %down_w.1, ...), custom_call_target="tpu_custom_call" | custom-call | tf_op jit(solution)/shard_map/pallas_call | solution.py:448
  73.1 2.1 %shard_map.103 = (bf16[256,1536]{1,0:T(8,128)(2,1)}, f32[12,192]{1,0:T(8,128)}, f32[12,192]{1,0:T(8,128)}, f32[12,192]{1,0:T(8,128)}) custom-call(bf16[256,1536]{1,0:T(8,128)(2,1)} %get-tuple-element.6.branch_in, f32[12,576]{1,0:T(8,128)} %get-tuple-element.7.owned_in), custom_call_target="tpu_custom_call" | custom-call | tf_op jit(solution)/shard_map/pallas_call | solution.py:460

commit v5 on v4

--- a/solution.py
+++ b/solution.py
@@ -53,7 +53,6 @@
         self.far = Z // 4
         self.comb = 4 * own
         self.pair = CORES * own
-        self.pairpad = ceil16(self.pair)
         self.cols = 3 * units
         self.half = Z // 2 * self.pair
         self.yrow = rows // Y
@@ -61,16 +60,16 @@
 
 def kernel(
     cfg,
-    lengths, send_order, frames, value_w, gate_w, down_w, cotangent,
+    lengths, send_order, frames_all, value_w, gate_w, down_w, cotangent_all,
     branch, owned,
-    out1, in1, out2, moved, normed, cot, glu_rows,
+    frames, cotangent, out1, in1, out2, moved, normed, cot, glu_rows,
     shards, w_own, w_sib, weights,
     block, pair_out, pair_in, x_out, x_in, near_out, near_in, acc, far_out, far_in, final,
     y_own, y_out, y_in, result,
     s_a1, r_a1, s_a2, r_a2, s_ag, r_ag,
     s_wf, r_wf, s_wn, r_wn, s_wx, r_wx, s_sib, r_sib,
     s_pair, r_pair, s_x, r_x, s_near, r_near, s_far, r_far, s_fin, r_fin, s_y, r_y, s_yg, r_yg,
-    relay,
+    relay, s_in,
 ):
     X, Z, Y, G = cfg.X, cfg.Z, cfg.Y, cfg.G
     R, U, F, cap = cfg.rows, cfg.units, cfg.far, cfg.cap
@@ -118,6 +117,12 @@
     for who in partners:
         pl.semaphore_signal(barrier, inc=1, device_id=who, device_id_type=pl.DeviceIdType.MESH)
 
+    columns = pl.ds(pl.multiple_of(y * cfg.part, 128), cfg.part)
+    get_frames = pltpu.make_async_copy(frames_all.at[:, columns], frames, s_in.at[0])
+    get_frames.start()
+    get_cotangent = pltpu.make_async_copy(cotangent_all, cotangent, s_in.at[1])
+    get_cotangent.start()
+
     packed = jnp.concatenate([value_w[...], gate_w[...], down_w[...]], axis=1)
     mine = shards.at[0, cfg.pad : 2 * cfg.pad]
     mine[...] = jnp.zeros_like(mine)
@@ -129,8 +134,8 @@
     numbers = jnp.broadcast_to(send_order[...].astype(F32).astype(BF), (16, R))
     order = dot(numbers, onehot(row == natural))[0:1, :]
     pick = onehot((row.astype(F32) == order) & (row < lengths[0]))
-    columns = pl.ds(pl.multiple_of(y * cfg.part, 128), cfg.part)
-    out1[...] = contract_rows(pick, frames[:, columns]).astype(BF)
+    get_frames.wait()
+    out1[...] = contract_rows(pick, frames[...]).astype(BF)
 
     pl.semaphore_wait(barrier, len(partners))
     for o in (4, -4):
@@ -213,6 +218,7 @@
         (lax.div(g_at, CORES) * Z + lax.rem(z + away, Z)) * CORES + lax.rem(g_at, CORES)
     ) * cap + k_at
     back = onehot(row == natural)
+    get_cotangent.wait()
     cot[...] = contract_rows(back, cotangent[...]).astype(BF)
 
     def share(j):
@@ -299,11 +305,26 @@
 
     glu_rows[...] = dot(back, glu).astype(BF)
     B = cfg.yrow
+    half_b = B // 2
     for d in (2, 1, 3):
-        mine_y = rows_of(glu_rows, mod(y + d, Y) * B, B)
-        y_out[d - 1] = contract_cols(mine_y[...], weights[:, 2 * U : 3 * U]).astype(BF)
-        send(y_out.at[d - 1], y_in.at[d - 1], s_y, r_y, at_y(d))
+        some = rows_of(glu_rows, mod(y + d, Y) * B, B)[...]
+        theirs = contract_cols(some, weights[:, 2 * U : 3 * U]).astype(BF)
+        for h in range(2):
+            y_out[h, d - 1] = theirs[h * half_b : (h + 1) * half_b]
+    for h in range(2):
+        for d in (2, 1, 3):
+            send(y_out.at[h, d - 1], y_in.at[h, d - 1], s_y, r_y.at[h], at_y(d))
     y_own[...] = contract_cols(rows_of(glu_rows, y * B, B)[...], weights[:, 2 * U : 3 * U])
+
+    def gather(h):
+        drain(r_y.at[h], y_in.at[h])
+        lines = y_own[h * half_b : (h + 1) * half_b, :]
+        for k in range(Y - 1):
+            lines = lines + y_in[h, k].astype(F32)
+        ref = rows_of(result, y * B + h * half_b, half_b)
+        ref[...] = lines.astype(BF)
+        for d in (2, 1, 3):
+            send(ref, ref, s_yg, r_yg, at_y(d))
 
     for o in (2, 1, 3):
         drain(r_pair.at[o], pair_in.at[o])
@@ -324,16 +345,10 @@
         near_out[i] = summed(i, steps[i]).astype(BF)
         send(near_out.at[i], near_in.at[i], s_near, r_near, at_z(steps[i]))
 
+    gather(0)
     to_near(0)
-
-    drain(r_y, y_in)
-    rows_of(result, y * B, B)[...] = (
-        y_own[...] + y_in[0].astype(F32) + y_in[1].astype(F32) + y_in[2].astype(F32)
-    ).astype(BF)
-    for d in (2, 1, 3):
-        send(rows_of(result, y * B, B), rows_of(result, y * B, B), s_yg, r_yg, at_y(d))
-
     to_near(1)
+    gather(1)
     to_near(2)
     total = summed(3, 0)
     drain(r_near, near_in)
@@ -342,44 +357,47 @@
 
     far_out[...] = jnp.zeros_like(far_out)
     sends = []
+    O = cfg.own
     for j in range(J):
-        part = total[j * Q : (j + 1) * Q]
-        acc[j] = part
-        far_out[j, 0:Q, :] = part.astype(BF)
         t = core * (Z // 2) + 4 * j + lax.rem(z, 4)
         slot = lax.div(mod(z - t, Z), 4)
-        copy = pltpu.make_async_remote_copy(
-            src_ref=far_out.at[j], dst_ref=far_in.at[slot], send_sem=s_far.at[j], recv_sem=r_far,
-            device_id=at(x, t, core), device_id_type=pl.DeviceIdType.MESH,
-        )
-        sends.append((t != z, copy))
-        pl.when(t != z)(copy.start)
+        for c in range(CORES):
+            lines = total[j * Q + c * O : j * Q + (c + 1) * O]
+            acc[j, c, 0:O, :] = lines
+            far_out[j, c, 0:O, :] = lines.astype(BF)
+            copy = pltpu.make_async_remote_copy(
+                src_ref=far_out.at[j, c], dst_ref=far_in.at[slot], send_sem=s_far.at[j, c], recv_sem=r_far,
+                device_id=at(x, t, c), device_id_type=pl.DeviceIdType.MESH,
+            )
+            sends.append((t != z, copy))
+            pl.when(t != z)(copy.start)
 
     is_owner = lax.div(z, Z // 2) == core
+    own_j = lax.rem(lax.div(z, 4), J)
     hand = pltpu.make_async_remote_copy(
-        src_ref=final, dst_ref=final, send_sem=s_fin, recv_sem=r_fin,
+        src_ref=acc.at[own_j, other], dst_ref=final, send_sem=s_fin, recv_sem=r_fin,
         device_id=sibling, device_id_type=pl.DeviceIdType.MESH,
     )
 
     @pl.when(is_owner)
     def _():
-        whole = acc[lax.rem(lax.div(z, 4), J)]
-        drain(r_far, far_in.at[1:F])
-        for slot in range(1, F):
-            whole = whole + far_in[slot, 0:Q, :].astype(F32)
-        final[...] = whole
         hand.start()
+        final[...] = acc[own_j, core]
         hand.wait_send()
 
     @pl.when(jnp.logical_not(is_owner))
     def _():
         hand.wait_recv()
 
-    whole = final[...]
-    owned[...] = jnp.where(core == 0, whole[0 : cfg.own], whole[cfg.own : 2 * cfg.own])
+    drain(r_far, far_in.at[1:F])
+    whole = final[0:O, :]
+    for slot in range(1, F):
+        whole = whole + far_in[slot, 0:O, :].astype(F32)
+    owned[...] = whole
 
     drain(r_yg, result.at[0 : (Y - 1) * B])
-    branch[...] = result[...]
+    put = pltpu.make_async_copy(result, branch, s_in.at[0])
+    put.start()
 
     drain(s_a1, out1.at[0 : (G - 1) * cfg.grow])
     drain(s_a2, out2.at[0 : (Z - 1) * cfg.zrow])
@@ -395,22 +413,35 @@
     drain(s_yg, result.at[0 : (Y - 1) * B])
     for needed, copy in sends:
         pl.when(needed)(copy.wait_send)
-
-
-def place_results(units, branch_in, owned_in, branch, grad_value, grad_gate, grad_down):
-    branch[...] = branch_in[...]
+    put.wait()
+
+
+def place_results(units, pieces, branch_in, owned_in, branch, grad_value, grad_gate, grad_down, sems):
+    size = branch_in.shape[0] // pieces
+    copies = [
+        pltpu.make_async_copy(
+            branch_in.at[i * size : (i + 1) * size], branch.at[i * size : (i + 1) * size], sems.at[i]
+        )
+        for i in range(pieces)
+    ]
+    for copy in copies:
+        copy.start()
     grad_value[...] = owned_in[:, :units]
     grad_gate[...] = owned_in[:, units : 2 * units]
     grad_down[...] = owned_in[:, 2 * units :]
+    for copy in copies:
+        copy.wait()
 
 
 def module(cfg, frames, lengths, send_order, value_weight, gate_weight, down_weight, cotangent):
     X, Z, Y, G, R, D, U = cfg.X, cfg.Z, cfg.Y, cfg.G, cfg.rows, cfg.width, cfg.units
     C, S, B = cfg.cols, cfg.half, cfg.yrow
-    vmem = pl.BlockSpec(memory_space=pltpu.VMEM)
+    vmem, hbm = pl.BlockSpec(memory_space=pltpu.VMEM), pl.BlockSpec(memory_space=pl.ANY)
     sem = pltpu.SemaphoreType.DMA
     F, J, H = cfg.far, Z // 8, Z // 8 * cfg.pair
     buffers = [
+        ((R, cfg.part), BF),
+        ((R, D), BF),
         ((R, cfg.part), BF),
         ((R, cfg.part), BF),
         ((R, cfg.part), BF),
@@ -429,39 +460,41 @@
         ((4, X - 1, H, C), BF),
         ((3, H, C), BF),
         ((3, H, C), BF),
-        ((J, cfg.pair, C), F32),
-        ((J, cfg.pairpad, C), BF),
-        ((F, cfg.pairpad, C), BF),
-        ((cfg.pair, C), F32),
+        ((J, CORES, cfg.pad, C), F32),
+        ((J, CORES, cfg.pad, C), BF),
+        ((F, cfg.pad, C), BF),
+        ((cfg.pad, C), F32),
         ((B, D), F32),
-        ((Y - 1, B, D), BF),
-        ((Y - 1, B, D), BF),
+        ((2, Y - 1, B // 2, D), BF),
+        ((2, Y - 1, B // 2, D), BF),
         ((R, D), BF),
     ]
     one = ()
     sems = [
         one, one, one, (4,), one, (4,),
         one, (F,), one, (F,), one, (F,), one, one,
-        one, (X,), one, (4,), one, one, (J,), one, one, one,
-        one, one, one, one,
+        one, (X,), one, (4,), one, one, (J, CORES), one, one, one,
+        one, (2,), one, one,
     ]
     branch, owned = pl.pallas_call(
         functools.partial(kernel, cfg),
         out_shape=(jax.ShapeDtypeStruct((R, D), BF), jax.ShapeDtypeStruct((cfg.own, C), F32)),
-        in_specs=[pl.BlockSpec(memory_space=pltpu.SMEM)] + [vmem] * 6,
-        out_specs=(vmem,) * 2,
+        in_specs=[pl.BlockSpec(memory_space=pltpu.SMEM), vmem, hbm, vmem, vmem, vmem, hbm],
+        out_specs=(hbm, vmem),
         scratch_shapes=[pltpu.VMEM(shape, kind) for shape, kind in buffers]
         + [sem(n) for n in sems]
-        + [pltpu.SemaphoreType.REGULAR],
+        + [pltpu.SemaphoreType.REGULAR, sem((2,))],
         compiler_params=pltpu.CompilerParams(
             collective_id=0, has_side_effects=True, vmem_limit_bytes=56 * 1024 * 1024
         ),
     )(lengths, send_order, frames, value_weight, gate_weight, down_weight, cotangent)
+    pieces = 8
     return pl.pallas_call(
-        functools.partial(place_results, U),
+        functools.partial(place_results, U, pieces),
         out_shape=(jax.ShapeDtypeStruct((R, D), BF),) + (jax.ShapeDtypeStruct((cfg.own, U), F32),) * 3,
-        in_specs=[vmem] * 2,
-        out_specs=(vmem,) * 4,
+        in_specs=[hbm, vmem],
+        out_specs=(hbm,) + (vmem,) * 3,
+        scratch_shapes=[sem((pieces,))],
     )(branch, owned)
 
 

time: 75.4 us -> 98.7 us (1.31)
  Pallas kernels: 73.9 us -> 97.1 us
    pallas_call x1, Pallas kernels: 2.07 us -> 26.4 us  [module(): pl.pallas_call(functools.partial(place_results, U, pieces), out_shape=(ja...]
    pallas_call x1, Pallas kernels: 71.9 us -> 70.7 us  [module(): pl.pallas_call(functools.partial(kernel, cfg), out_shape=(jax.ShapeDtypeS...]
where the time goes in v5:
time: 98.7 us; the launch traced here: 98.4 us
  Pallas kernels  97.1 us (98%)
  between operations  1.29 us (1%)
    pallas_call x1, Pallas kernels, module(): pl.pallas_call(functools.partial(kernel, cfg), out_shape=(jax.ShapeDtypeS...  70.7 us
    pallas_call x1, Pallas kernels, module(): pl.pallas_call(functools.partial(place_results, U, pieces), out_shape=(ja...  26.4 us

profile of v5, /device:TPU:1, one launch (start us, length us, event | category | flops | bytes accessed | tf_op | source)
XLA Modules:
  0.0 98.4 jit_solution(11613615613368515073)
XLA Ops:
  1.3 70.7 %shard_map.102 = (bf16[256,1536]{1,0:T(8,128)(2,1)}, f32[12,576]{1,0:T(8,128)}) custom-call(s32[1]{0:T(128)S(6)} %copy.11.lengths, s32[1,256]{1,0:T(1,128)} %send_order.1, bf16[256,1536]{1,0:T(8,128)(2,1)} %frames_all.1, bf16[12,192]{1,0:T(8,128)(2,1)} %value_w.1, bf16[12,192]{1,0:T(8,128)(2,1)} %gate_w.1, bf16[12,192]{1,0:T(8,128)(2,1)} %down_w.1, ...), custom_call_target="tpu_custom_call" | custom-call | tf_op jit(solution)/shard_map/pallas_call | solution.py:479
  72.0 26.4 %shard_map.103 = (bf16[256,1536]{1,0:T(8,128)(2,1)}, f32[12,192]{1,0:T(8,128)}, f32[12,192]{1,0:T(8,128)}, f32[12,192]{1,0:T(8,128)}) custom-call(bf16[256,1536]{1,0:T(8,128)(2,1)} %get-tuple-element.6.branch_in, f32[12,576]{1,0:T(8,128)} %get-tuple-element.7.owned_in), custom_call_target="tpu_custom_call" | custom-call | tf_op jit(solution)/shard_map/pallas_call | solution.py:492

commit v6 on v5

--- a/solution.py
+++ b/solution.py
@@ -69,7 +69,7 @@
     s_a1, r_a1, s_a2, r_a2, s_ag, r_ag,
     s_wf, r_wf, s_wn, r_wn, s_wx, r_wx, s_sib, r_sib,
     s_pair, r_pair, s_x, r_x, s_near, r_near, s_far, r_far, s_fin, r_fin, s_y, r_y, s_yg, r_yg,
-    relay, s_in,
+    relay, s_in, s_put,
 ):
     X, Z, Y, G = cfg.X, cfg.Z, cfg.Y, cfg.G
     R, U, F, cap = cfg.rows, cfg.units, cfg.far, cfg.cap
@@ -324,7 +324,15 @@
         ref = rows_of(result, y * B + h * half_b, half_b)
         ref[...] = lines.astype(BF)
         for d in (2, 1, 3):
-            send(ref, ref, s_yg, r_yg, at_y(d))
+            send(ref, ref, s_yg, r_yg.at[h], at_y(d))
+
+    def put_out(h):
+        drain(r_yg.at[h], result.at[0 : (Y - 1) * half_b])
+        for i in range(Y):
+            lo = i * B + h * half_b
+            pltpu.make_async_copy(
+                result.at[lo : lo + half_b], branch.at[lo : lo + half_b], s_put
+            ).start()
 
     for o in (2, 1, 3):
         drain(r_pair.at[o], pair_in.at[o])
@@ -389,15 +397,14 @@
     def _():
         hand.wait_recv()
 
+    put_out(0)
     drain(r_far, far_in.at[1:F])
     whole = final[0:O, :]
     for slot in range(1, F):
         whole = whole + far_in[slot, 0:O, :].astype(F32)
     owned[...] = whole
 
-    drain(r_yg, result.at[0 : (Y - 1) * B])
-    put = pltpu.make_async_copy(result, branch, s_in.at[0])
-    put.start()
+    put_out(1)
 
     drain(s_a1, out1.at[0 : (G - 1) * cfg.grow])
     drain(s_a2, out2.at[0 : (Z - 1) * cfg.zrow])
@@ -413,24 +420,14 @@
     drain(s_yg, result.at[0 : (Y - 1) * B])
     for needed, copy in sends:
         pl.when(needed)(copy.wait_send)
-    put.wait()
-
-
-def place_results(units, pieces, branch_in, owned_in, branch, grad_value, grad_gate, grad_down, sems):
-    size = branch_in.shape[0] // pieces
-    copies = [
-        pltpu.make_async_copy(
-            branch_in.at[i * size : (i + 1) * size], branch.at[i * size : (i + 1) * size], sems.at[i]
-        )
-        for i in range(pieces)
-    ]
-    for copy in copies:
-        copy.start()
+    drain(s_put, result)
+
+
+def place_results(units, branch_in, owned_in, branch, grad_value, grad_gate, grad_down):
+    branch[...] = branch_in[...]
     grad_value[...] = owned_in[:, :units]
     grad_gate[...] = owned_in[:, units : 2 * units]
     grad_down[...] = owned_in[:, 2 * units :]
-    for copy in copies:
-        copy.wait()
 
 
 def module(cfg, frames, lengths, send_order, value_weight, gate_weight, down_weight, cotangent):
@@ -474,7 +471,7 @@
         one, one, one, (4,), one, (4,),
         one, (F,), one, (F,), one, (F,), one, one,
         one, (X,), one, (4,), one, one, (J, CORES), one, one, one,
-        one, (2,), one, one,
+        one, (2,), one, (2,),
     ]
     branch, owned = pl.pallas_call(
         functools.partial(kernel, cfg),
@@ -483,18 +480,16 @@
         out_specs=(hbm, vmem),
         scratch_shapes=[pltpu.VMEM(shape, kind) for shape, kind in buffers]
         + [sem(n) for n in sems]
-        + [pltpu.SemaphoreType.REGULAR, sem((2,))],
+        + [pltpu.SemaphoreType.REGULAR, sem((2,)), sem(one)],
         compiler_params=pltpu.CompilerParams(
             collective_id=0, has_side_effects=True, vmem_limit_bytes=56 * 1024 * 1024
         ),
     )(lengths, send_order, frames, value_weight, gate_weight, down_weight, cotangent)
-    pieces = 8
     return pl.pallas_call(
-        functools.partial(place_results, U, pieces),
+        functools.partial(place_results, U),
         out_shape=(jax.ShapeDtypeStruct((R, D), BF),) + (jax.ShapeDtypeStruct((cfg.own, U), F32),) * 3,
-        in_specs=[hbm, vmem],
-        out_specs=(hbm,) + (vmem,) * 3,
-        scratch_shapes=[sem((pieces,))],
+        in_specs=[vmem] * 2,
+        out_specs=(vmem,) * 4,
     )(branch, owned)
 
 

time: 98.7 us -> 74.2 us (0.75)
  Pallas kernels: 97.1 us -> 72.7 us
    pallas_call x1, Pallas kernels: 26.4 us -> 2.07 us  [module(): pl.pallas_call(functools.partial(place_results, U), out_shape=(jax.ShapeD...]
where the time goes in v6:
time: 74.2 us; the launch traced here: 74 us
  Pallas kernels  72.7 us (98%)
  between operations  1.29 us (2%)
    pallas_call x1, Pallas kernels, module(): pl.pallas_call(functools.partial(kernel, cfg), out_shape=(jax.ShapeDtypeS...  70.6 us
    pallas_call x1, Pallas kernels, module(): pl.pallas_call(functools.partial(place_results, U), out_shape=(jax.ShapeD...  2.07 us

profile of v6, /device:TPU:1, one launch (start us, length us, event | category | flops | bytes accessed | tf_op | source)
XLA Modules:
  0.0 74.0 jit_solution(8457628625694163478)
XLA Ops:
  1.3 70.6 %shard_map.102 = (bf16[256,1536]{1,0:T(8,128)(2,1)}, f32[12,576]{1,0:T(8,128)}) custom-call(s32[1]{0:T(128)S(6)} %copy.11.lengths, s32[1,256]{1,0:T(1,128)} %send_order.1, bf16[256,1536]{1,0:T(8,128)(2,1)} %frames_all.1, bf16[12,192]{1,0:T(8,128)(2,1)} %value_w.1, bf16[12,192]{1,0:T(8,128)(2,1)} %gate_w.1, bf16[12,192]{1,0:T(8,128)(2,1)} %down_w.1, ...), custom_call_target="tpu_custom_call" | custom-call | tf_op jit(solution)/shard_map/pallas_call | solution.py:476
  71.9 2.1 %shard_map.103 = (bf16[256,1536]{1,0:T(8,128)(2,1)}, f32[12,192]{1,0:T(8,128)}, f32[12,192]{1,0:T(8,128)}, f32[12,192]{1,0:T(8,128)}) custom-call(bf16[256,1536]{1,0:T(8,128)(2,1)} %get-tuple-element.6.branch_in, f32[12,576]{1,0:T(8,128)} %get-tuple-element.7.owned_in), custom_call_target="tpu_custom_call" | custom-call | tf_op jit(solution)/shard_map/pallas_call | solution.py:488

commit v7 on v6

--- a/solution.py
+++ b/solution.py
@@ -54,8 +54,41 @@
         self.comb = 4 * own
         self.pair = CORES * own
         self.cols = 3 * units
+        self.main = self.cols // 128 * 128
+        self.fold = own // (self.pad - own)
         self.half = Z // 2 * self.pair
         self.yrow = rows // Y
+
+
+def pack(cfg, lines):
+    own, pad, main, fold = cfg.own, cfg.pad, cfg.main, cfg.fold
+    count = lines.shape[0] // own
+    q = iota((1, count * own), 1)
+    m, r = lax.div(q, own), lax.rem(q, own)
+    p = iota((count * pad, count * own), 0)
+    body = dot(onehot(p == m * pad + r), lines[:, :main])
+    tails = [
+        dot(onehot(p == jnp.where(lax.rem(r, fold) == s, m * pad + own + lax.div(r, fold), -1)), lines[:, main:])
+        for s in range(fold)
+    ]
+    wide = -(-fold * (cfg.cols - main) // 128) * 128
+    tails.append(jnp.zeros((count * pad, wide - fold * (cfg.cols - main)), F32))
+    tail = jnp.concatenate(tails, axis=1)
+    return jnp.concatenate([body[:, :wide] + tail, body[:, wide:]], axis=1).astype(BF)
+
+
+def unpack(cfg, lines):
+    own, pad, main, fold = cfg.own, cfg.pad, cfg.main, cfg.fold
+    count, rest = lines.shape[0] // pad, cfg.cols - main
+    q = iota((1, count * pad), 1)
+    m, r = lax.div(q, pad), lax.rem(q, pad)
+    p = iota((count * own, count * pad), 0)
+    body = dot(onehot(p == jnp.where(r < own, m * own + r, -1)), lines)
+    tail = sum(
+        dot(onehot(p == jnp.where(r < own, -1, m * own + (r - own) * fold + s)), lines[:, s * rest : (s + 1) * rest])
+        for s in range(fold)
+    )
+    return jnp.concatenate([body, tail], axis=1).astype(BF)
 
 
 def kernel(
@@ -64,11 +97,11 @@
     branch, owned,
     frames, cotangent, out1, in1, out2, moved, normed, cot, glu_rows,
     shards, w_own, w_sib, weights,
-    block, pair_out, pair_in, x_out, x_in, near_out, near_in, acc, far_out, far_in, final,
+    block, pair_out, pair_in, x_out, x_in, z_out, z_in, acc, final,
     y_own, y_out, y_in, result,
     s_a1, r_a1, s_a2, r_a2, s_ag, r_ag,
     s_wf, r_wf, s_wn, r_wn, s_wx, r_wx, s_sib, r_sib,
-    s_pair, r_pair, s_x, r_x, s_near, r_near, s_far, r_far, s_fin, r_fin, s_y, r_y, s_yg, r_yg,
+    s_pair, r_pair, s_x, r_x, s_z, r_z, s_own, s_fin, r_fin, s_y, r_y, s_yg, r_yg,
     relay, s_in, s_put,
 ):
     X, Z, Y, G = cfg.X, cfg.Z, cfg.Y, cfg.G
@@ -125,8 +158,7 @@
 
     packed = jnp.concatenate([value_w[...], gate_w[...], down_w[...]], axis=1)
     mine = shards.at[0, cfg.pad : 2 * cfg.pad]
-    mine[...] = jnp.zeros_like(mine)
-    shards[0, cfg.pad : cfg.pad + cfg.own, :] = packed
+    mine[...] = pack(cfg, packed)
 
     row, place = iota((R, R), 0), iota((1, R), 1)
     k_of, z_of, g_of = lax.rem(place, cap), lax.rem(lax.div(place, cap), Z), lax.div(place, cap * Z)
@@ -188,15 +220,9 @@
     to_z((0, 1))
     here[0 : cfg.zrow, :] = rows_of(out2, z * cfg.zrow, cfg.zrow)[...]
 
-    q = iota((1, 4 * cfg.pad), 1)
-    j = lax.rem(q, cfg.pad)
-    squeeze = onehot(
-        iota((cfg.comb, 4 * cfg.pad), 0) == jnp.where(j < cfg.own, lax.div(q, cfg.pad) * cfg.own + j, -1)
-    )
-
     def spread(f):
         drain(r_wn.at[f], shards.at[f, 0 : 3 * cfg.pad])
-        w_own[f, 0] = dot(squeeze, shards[f]).astype(BF)
+        w_own[f, 0] = unpack(cfg, shards[f])
         for k in (2, 1, 3):
             send(w_own.at[f, 0], w_own.at[f, k], s_wx, r_wx.at[f], at_x(k))
 
@@ -285,7 +311,7 @@
 
     d_both = jnp.concatenate([d_value, d_gate], axis=1)
     J = Z // 2 // 4
-    steps = (2, 1, -1, 0)
+    steps = (0, 1, -1, 2)
     Q = cfg.pair
 
     def chunk(o, half, a):
@@ -349,36 +375,35 @@
             total = total + x_in[i, k].astype(F32)
         return total
 
-    def to_near(i):
-        near_out[i] = summed(i, steps[i]).astype(BF)
-        send(near_out.at[i], near_in.at[i], s_near, r_near, at_z(steps[i]))
-
+    O = cfg.own
+    sends = []
+
+    def to_owners(i):
+        a = steps[i]
+        total = summed(i, a)
+        z_out[i] = pack(cfg, total.astype(BF))
+        for j in range(J):
+            t = core * (Z // 2) + 4 * j + lax.rem(z + a + Z, 4)
+            for c in range(CORES):
+                lo = j * CORES + c
+                copy = pltpu.make_async_remote_copy(
+                    src_ref=z_out.at[i, lo * cfg.pad : (lo + 1) * cfg.pad], dst_ref=z_in.at[mod(z - t, Z)],
+                    send_sem=s_own.at[j, c] if a == 0 else s_z, recv_sem=r_z,
+                    device_id=at(x, t, c), device_id_type=pl.DeviceIdType.MESH,
+                )
+                if a == 0:
+                    acc[j, c, 0:O, :] = total[lo * O : (lo + 1) * O]
+                    sends.append((t != z, copy))
+                    pl.when(t != z)(copy.start)
+                else:
+                    copy.start()
+
+    to_owners(0)
     gather(0)
-    to_near(0)
-    to_near(1)
+    to_owners(1)
+    to_owners(2)
     gather(1)
-    to_near(2)
-    total = summed(3, 0)
-    drain(r_near, near_in)
-    for i in range(3):
-        total = total + near_in[i].astype(F32)
-
-    far_out[...] = jnp.zeros_like(far_out)
-    sends = []
-    O = cfg.own
-    for j in range(J):
-        t = core * (Z // 2) + 4 * j + lax.rem(z, 4)
-        slot = lax.div(mod(z - t, Z), 4)
-        for c in range(CORES):
-            lines = total[j * Q + c * O : j * Q + (c + 1) * O]
-            acc[j, c, 0:O, :] = lines
-            far_out[j, c, 0:O, :] = lines.astype(BF)
-            copy = pltpu.make_async_remote_copy(
-                src_ref=far_out.at[j, c], dst_ref=far_in.at[slot], send_sem=s_far.at[j, c], recv_sem=r_far,
-                device_id=at(x, t, c), device_id_type=pl.DeviceIdType.MESH,
-            )
-            sends.append((t != z, copy))
-            pl.when(t != z)(copy.start)
+    to_owners(3)
 
     is_owner = lax.div(z, Z // 2) == core
     own_j = lax.rem(lax.div(z, 4), J)
@@ -398,11 +423,17 @@
         hand.wait_recv()
 
     put_out(0)
-    drain(r_far, far_in.at[1:F])
-    whole = final[0:O, :]
-    for slot in range(1, F):
-        whole = whole + far_in[slot, 0:O, :].astype(F32)
-    owned[...] = whole
+    drain(r_z, z_in.at[1:Z])
+    whole = z_in[1].astype(F32)
+    for slot in range(2, Z):
+        whole = whole + z_in[slot].astype(F32)
+    rest = cfg.cols - cfg.main
+    tail = []
+    for r in range(O):
+        lo, line = r % cfg.fold * rest, O + r // cfg.fold
+        tail.append(whole[line : line + 1, lo : lo + rest])
+    whole = jnp.concatenate([whole[0:O], jnp.concatenate(tail, axis=0)], axis=1)
+    owned[...] = whole + final[0:O, :]
 
     put_out(1)
 
@@ -415,7 +446,7 @@
     drain(s_sib, w_own)
     drain(s_pair, pair_out)
     drain(s_x, x_out)
-    drain(s_near, near_out)
+    drain(s_z, z_out.at[1:4])
     drain(s_y, y_out)
     drain(s_yg, result.at[0 : (Y - 1) * B])
     for needed, copy in sends:
@@ -446,7 +477,7 @@
         ((R, D), BF),
         ((R, D), BF),
         ((R, U), BF),
-        ((F, 4 * cfg.pad, C), BF),
+        ((F, 4 * cfg.pad, cfg.main), BF),
         ((F, X, cfg.comb, C), BF),
         ((F, X, cfg.comb, C), BF),
         ((D, C), BF),
@@ -455,11 +486,9 @@
         ((X, 4, H, C), BF),
         ((4, X - 1, H, C), BF),
         ((4, X - 1, H, C), BF),
-        ((3, H, C), BF),
-        ((3, H, C), BF),
+        ((4, J * CORES * cfg.pad, cfg.main), BF),
+        ((Z, cfg.pad, cfg.main), BF),
         ((J, CORES, cfg.pad, C), F32),
-        ((J, CORES, cfg.pad, C), BF),
-        ((F, cfg.pad, C), BF),
         ((cfg.pad, C), F32),
         ((B, D), F32),
         ((2, Y - 1, B // 2, D), BF),
@@ -470,7 +499,7 @@
     sems = [
         one, one, one, (4,), one, (4,),
         one, (F,), one, (F,), one, (F,), one, one,
-        one, (X,), one, (4,), one, one, (J, CORES), one, one, one,
+        one, (X,), one, (4,), one, one, (J, CORES), one, one,
         one, (2,), one, (2,),
     ]
     branch, owned = pl.pallas_call(

time: 74.2 us -> 73.8 us (level)
  no operation moved by 1% of the time
where the time goes in v7:
time: 73.8 us; the launch traced here: 73.5 us
  Pallas kernels  72.3 us (98%)
  between operations  1.29 us (2%)
    pallas_call x1, Pallas kernels, module(): pl.pallas_call(functools.partial(kernel, cfg), out_shape=(jax.ShapeDtypeS...  70.2 us
    pallas_call x1, Pallas kernels, module(): pl.pallas_call(functools.partial(place_results, U), out_shape=(jax.ShapeD...  2.07 us

profile of v7, /device:TPU:1, one launch (start us, length us, event | category | flops | bytes accessed | tf_op | source)
XLA Modules:
  0.0 73.5 jit_solution(16957593032439940086)
XLA Ops:
  1.3 70.2 %shard_map.102 = (bf16[256,1536]{1,0:T(8,128)(2,1)}, f32[12,576]{1,0:T(8,128)}) custom-call(s32[1]{0:T(128)S(6)} %copy.11.lengths, s32[1,256]{1,0:T(1,128)} %send_order.1, bf16[256,1536]{1,0:T(8,128)(2,1)} %frames_all.1, bf16[12,192]{1,0:T(8,128)(2,1)} %value_w.1, bf16[12,192]{1,0:T(8,128)(2,1)} %gate_w.1, bf16[12,192]{1,0:T(8,128)(2,1)} %down_w.1, ...), custom_call_target="tpu_custom_call" | custom-call | tf_op jit(solution)/shard_map/pallas_call | solution.py:505
  71.5 2.1 %shard_map.103 = (bf16[256,1536]{1,0:T(8,128)(2,1)}, f32[12,192]{1,0:T(8,128)}, f32[12,192]{1,0:T(8,128)}, f32[12,192]{1,0:T(8,128)}) custom-call(bf16[256,1536]{1,0:T(8,128)(2,1)} %get-tuple-element.6.branch_in, f32[12,576]{1,0:T(8,128)} %get-tuple-element.7.owned_in), custom_call_target="tpu_custom_call" | custom-call | tf_op jit(solution)/shard_map/pallas_call | solution.py:517

commit v8 on v7

--- a/solution.py
+++ b/solution.py
@@ -204,17 +204,19 @@
     out2[...] = dot(onehot(row == to_new), in1[...]).astype(BF)
     here = moved.at[y]
     position = [0] + [2 * o - 1 if o <= Z // 2 else 2 * (Z - o) for o in range(1, Z)]
-    parcels = 4
-    each = R // parcels
-    per = each // cfg.zrow
+    quarter = Z // 4
+    edges = [0, quarter, 2 * quarter, 3 * quarter, Z - quarter // 2, Z]
+    parcel_of = [sum(p >= edge for edge in edges[1:]) for p in range(Z)]
+    bounds = [(lo * cfg.zrow, hi * cfg.zrow) for lo, hi in zip(edges, edges[1:])]
+
     def to_z(parcel_range):
         for o in sorted(range(1, Z), key=lambda o: position[Z - o]):
             p = position[Z - o]
-            if p // per in parcel_range:
+            if parcel_of[p] in parcel_range:
                 send(
                     rows_of(out2, mod(z + o, Z) * cfg.zrow, cfg.zrow),
                     here.at[p * cfg.zrow : (p + 1) * cfg.zrow],
-                    s_a2, r_a2.at[p // per], at_z(o),
+                    s_a2, r_a2.at[parcel_of[p]], at_z(o),
                 )
 
     to_z((0, 1))
@@ -232,10 +234,9 @@
 
     spread(0)
     for f in (1, 3, 2):
-        if f < F:
-            drain(r_wf.at[f], shards.at[f, cfg.pad : 2 * cfg.pad])
-            pass_near(f)
-    to_z((2, 3))
+        drain(r_wf.at[f], shards.at[f, cfg.pad : 2 * cfg.pad])
+        pass_near(f)
+    to_z((2, 3, 4))
 
     where = lax.div(place, cfg.zrow)
     away = jnp.where(lax.rem(where, 2) == 1, lax.div(where + 1, 2), lax.rem(Z - lax.div(where, 2), Z))
@@ -248,16 +249,18 @@
     cot[...] = contract_rows(back, cotangent[...]).astype(BF)
 
     def share(j):
-        drain(r_a2.at[j], here.at[(0 if j else cfg.zrow) : each])
-        ref = here.at[j * each : (j + 1) * each]
+        lo, hi = bounds[j]
+        drain(r_a2.at[j], here.at[(lo if j else cfg.zrow) : hi])
+        ref = here.at[lo:hi]
         for d in (2, 1, 3):
             send(ref, ref, s_ag, r_ag.at[j], at_y(d))
 
     def normalize(j):
-        drain(r_ag.at[j], moved.at[0, 0 : (Y - 1) * each])
-        lines = 32
-        for i in range(each // lines):
-            span = slice(j * each + i * lines, j * each + (i + 1) * lines)
+        start, stop = bounds[j]
+        drain(r_ag.at[j], moved.at[0, 0 : (Y - 1) * (stop - start)])
+        lines = min(32, stop - start)
+        for lo in range(start, stop, lines):
+            span = slice(lo, lo + lines)
             parts = [moved[c, span, :].astype(F32) for c in range(Y)]
             mean = sum(jnp.sum(p, axis=1, keepdims=True) for p in parts) / cfg.width
             parts = [p - mean for p in parts]
@@ -267,19 +270,18 @@
                 normed[span, c * cfg.part : (c + 1) * cfg.part] = (parts[c] * scale).astype(BF)
 
     share(0)
-    for f in (1, 3, 2):
-        if f < F:
-            spread(f)
-        if f == 3:
-            share(1)
+    spread(1)
+    spread(3)
+    share(1)
+    spread(2)
     hand_on(0)
     share(2)
     hand_on(1)
     normalize(0)
     share(3)
-    for f in (3, 2):
-        if f < F:
-            hand_on(f)
+    hand_on(3)
+    share(4)
+    hand_on(2)
     normalize(1)
     normalize(2)
 
@@ -301,6 +303,7 @@
 
     dglu = dot(cot[...], weights[:, 2 * U : 3 * U])
     normalize(3)
+    normalize(4)
 
     both = dot(normed[...], weights[:, : 2 * U])
     value, gate = both[:, :U], both[:, U : 2 * U]
@@ -329,9 +332,36 @@
             pair_out[o, i] = chunk(o, other, a).astype(BF)
         send(pair_out.at[o], pair_in.at[o], s_pair, r_pair.at[o], sibling)
 
-    glu_rows[...] = dot(back, glu).astype(BF)
     B = cfg.yrow
     half_b = B // 2
+
+    def gather(h):
+        drain(r_y.at[h], y_in.at[h])
+        lines = y_own[h * half_b : (h + 1) * half_b, :]
+        for k in range(Y - 1):
+            lines = lines + y_in[h, k].astype(F32)
+        ref = rows_of(result, y * B + h * half_b, half_b)
+        ref[...] = lines.astype(BF)
+        for d in (2, 1, 3):
+            send(ref, ref, s_yg, r_yg.at[h], at_y(d))
+
+    def put_out(h):
+        drain(r_yg.at[h], result.at[0 : (Y - 1) * half_b])
+        for i in range(Y):
+            lo = i * B + h * half_b
+            pltpu.make_async_copy(
+                result.at[lo : lo + half_b], branch.at[lo : lo + half_b], s_put
+            ).start()
+
+    def to_x(i, o):
+        x_out[i, o - 1] = (chunk(o, core, steps[i]) + pair_in[o, i].astype(F32)).astype(BF)
+        send(x_out.at[i, o - 1], x_in.at[i, o - 1], s_x, r_x.at[i], at_x(o))
+
+    for o in (2, 1, 3):
+        drain(r_pair.at[o], pair_in.at[o])
+        to_x(0, o)
+
+    glu_rows[...] = dot(back, glu).astype(BF)
     for d in (2, 1, 3):
         some = rows_of(glu_rows, mod(y + d, Y) * B, B)[...]
         theirs = contract_cols(some, weights[:, 2 * U : 3 * U]).astype(BF)
@@ -342,30 +372,9 @@
             send(y_out.at[h, d - 1], y_in.at[h, d - 1], s_y, r_y.at[h], at_y(d))
     y_own[...] = contract_cols(rows_of(glu_rows, y * B, B)[...], weights[:, 2 * U : 3 * U])
 
-    def gather(h):
-        drain(r_y.at[h], y_in.at[h])
-        lines = y_own[h * half_b : (h + 1) * half_b, :]
-        for k in range(Y - 1):
-            lines = lines + y_in[h, k].astype(F32)
-        ref = rows_of(result, y * B + h * half_b, half_b)
-        ref[...] = lines.astype(BF)
-        for d in (2, 1, 3):
-            send(ref, ref, s_yg, r_yg.at[h], at_y(d))
-
-    def put_out(h):
-        drain(r_yg.at[h], result.at[0 : (Y - 1) * half_b])
-        for i in range(Y):
-            lo = i * B + h * half_b
-            pltpu.make_async_copy(
-                result.at[lo : lo + half_b], branch.at[lo : lo + half_b], s_put
-            ).start()
-
-    for o in (2, 1, 3):
-        drain(r_pair.at[o], pair_in.at[o])
-    for i, a in enumerate(steps):
+    for i in range(1, 4):
         for o in (2, 1, 3):
-            x_out[i, o - 1] = (chunk(o, core, a) + pair_in[o, i].astype(F32)).astype(BF)
-            send(x_out.at[i, o - 1], x_in.at[i, o - 1], s_x, r_x.at[i], at_x(o))
+            to_x(i, o)
     drain(r_pair.at[0], pair_in.at[0])
 
     def summed(i, a):
@@ -497,7 +506,7 @@
     ]
     one = ()
     sems = [
-        one, one, one, (4,), one, (4,),
+        one, one, one, (5,), one, (5,),
         one, (F,), one, (F,), one, (F,), one, one,
         one, (X,), one, (4,), one, one, (J, CORES), one, one,
         one, (2,), one, (2,),

time: 73.8 us -> 72.5 us (0.982)
  Pallas kernels: 72.3 us -> 71 us
    pallas_call x1, Pallas kernels: 70.2 us -> 68.9 us  [module(): pl.pallas_call(functools.partial(kernel, cfg), out_shape=(jax.ShapeDtypeS...]
where the time goes in v8:
time: 72.5 us; the launch traced here: 72.2 us
  Pallas kernels  71 us (98%)
  between operations  1.29 us (2%)
    pallas_call x1, Pallas kernels, module(): pl.pallas_call(functools.partial(kernel, cfg), out_shape=(jax.ShapeDtypeS...  68.9 us
    pallas_call x1, Pallas kernels, module(): pl.pallas_call(functools.partial(place_results, U), out_shape=(jax.ShapeD...  2.07 us

profile of v8, /device:TPU:1, one launch (start us, length us, event | category | flops | bytes accessed | tf_op | source)
XLA Modules:
  0.0 72.2 jit_solution(6105928650440166753)
XLA Ops:
  1.3 68.9 %shard_map.102 = (bf16[256,1536]{1,0:T(8,128)(2,1)}, f32[12,576]{1,0:T(8,128)}) custom-call(s32[1]{0:T(128)S(6)} %copy.11.lengths, s32[1,256]{1,0:T(1,128)} %send_order.1, bf16[256,1536]{1,0:T(8,128)(2,1)} %frames_all.1, bf16[12,192]{1,0:T(8,128)(2,1)} %value_w.1, bf16[12,192]{1,0:T(8,128)(2,1)} %gate_w.1, bf16[12,192]{1,0:T(8,128)(2,1)} %down_w.1, ...), custom_call_target="tpu_custom_call" | custom-call | tf_op jit(solution)/shard_map/pallas_call | solution.py:514
  70.2 2.1 %shard_map.103 = (bf16[256,1536]{1,0:T(8,128)(2,1)}, f32[12,192]{1,0:T(8,128)}, f32[12,192]{1,0:T(8,128)}, f32[12,192]{1,0:T(8,128)}) custom-call(bf16[256,1536]{1,0:T(8,128)(2,1)} %get-tuple-element.6.branch_in, f32[12,576]{1,0:T(8,128)} %get-tuple-element.7.owned_in), custom_call_target="tpu_custom_call" | custom-call | tf_op jit(solution)/shard_map/pallas_call | solution.py:526

commit v9 on v8

--- a/solution.py
+++ b/solution.py
@@ -96,8 +96,8 @@
     lengths, send_order, frames_all, value_w, gate_w, down_w, cotangent_all,
     branch, owned,
     frames, cotangent, out1, in1, out2, moved, normed, cot, glu_rows,
-    shards, w_own, w_sib, weights,
-    block, pair_out, pair_in, x_out, x_in, z_out, z_in, acc, final,
+    shards, w_own, w_sib, staged, weights,
+    block, pair_out, pair_in, x_out, x_in, z_out, z_in, acc, final, last,
     y_own, y_out, y_in, result,
     s_a1, r_a1, s_a2, r_a2, s_ag, r_ag,
     s_wf, r_wf, s_wn, r_wn, s_wx, r_wx, s_sib, r_sib,
@@ -230,7 +230,7 @@
 
     def hand_on(f):
         drain(r_wx.at[f], w_own.at[f, 1:X])
-        send(w_own.at[f], w_sib.at[f], s_sib, r_sib, sibling)
+        send(w_own.at[f], w_sib.at[f], s_sib, r_sib.at[f], sibling)
 
     spread(0)
     for f in (1, 3, 2):
@@ -268,6 +268,21 @@
             scale = lax.rsqrt(var + 1e-05)
             for c in range(Y):
                 normed[span, c * cfg.part : (c + 1) * cfg.part] = (parts[c] * scale).astype(BF)
+
+    q = iota((1, CORES * cfg.comb), 1)
+    side = lax.div(q, cfg.comb)
+    core_of = core + side - 2 * core * side
+    line = lax.div(lax.rem(q, cfg.comb), cfg.own) * cfg.pair + core_of * cfg.own + lax.rem(q, cfg.own)
+    spot = onehot(iota((CORES * cfg.comb, CORES * cfg.comb), 0) == line)
+    span = Z * cfg.pair
+
+    def put_weights(f):
+        drain(r_sib.at[f], w_sib.at[f])
+        for k in range(X):
+            lines = dot(spot, jnp.concatenate([w_own[f, k], w_sib[f, k]], axis=0))
+            for n in range(4):
+                chip = mod(x - k, X) * Z + lax.rem(z - (n - 1) - 4 * f + 2 * Z, Z)
+                rows_of(staged, chip * cfg.pair, cfg.pair, 8)[...] = lines[n * cfg.pair : (n + 1) * cfg.pair]
 
     share(0)
     spread(1)
@@ -283,23 +298,12 @@
     share(4)
     hand_on(2)
     normalize(1)
+    put_weights(0)
+    put_weights(1)
     normalize(2)
-
-    q = iota((1, 2 * F * cfg.comb), 1)
-    side = lax.div(q, F * cfg.comb)
-    f_of = lax.rem(lax.div(q, cfg.comb), F)
-    n_of = lax.rem(lax.div(q, cfg.own), 4)
-    z_of = lax.rem(z - (n_of - 1) - 4 * f_of + 2 * Z, Z)
-    core_of = core + side - 2 * core * side
-    natural = (z_of * CORES + core_of) * cfg.own + lax.rem(q, cfg.own)
-    span = Z * cfg.pair
-    spot = onehot(iota((span, span), 0) == natural)
-    drain(r_sib, w_sib)
-    for k in range(X):
-        pieces = [w[f, k] for w in (w_own, w_sib) for f in range(F)]
-        rows_of(weights, mod(x - k, X) * span, span)[...] = dot(
-            spot, jnp.concatenate(pieces, axis=0)
-        ).astype(BF)
+    put_weights(3)
+    put_weights(2)
+    weights[...] = staged[...].astype(BF)
 
     dglu = dot(cot[...], weights[:, 2 * U : 3 * U])
     normalize(3)
@@ -442,7 +446,9 @@
         lo, line = r % cfg.fold * rest, O + r // cfg.fold
         tail.append(whole[line : line + 1, lo : lo + rest])
     whole = jnp.concatenate([whole[0:O], jnp.concatenate(tail, axis=0)], axis=1)
-    owned[...] = whole + final[0:O, :]
+    last[...] = whole + final[0:O, :]
+    put_last = pltpu.make_async_copy(last, owned, s_in.at[0])
+    put_last.start()
 
     put_out(1)
 
@@ -461,6 +467,7 @@
     for needed, copy in sends:
         pl.when(needed)(copy.wait_send)
     drain(s_put, result)
+    put_last.wait()
 
 
 def place_results(units, branch_in, owned_in, branch, grad_value, grad_gate, grad_down):
@@ -489,6 +496,7 @@
         ((F, 4 * cfg.pad, cfg.main), BF),
         ((F, X, cfg.comb, C), BF),
         ((F, X, cfg.comb, C), BF),
+        ((D, C), F32),
         ((D, C), BF),
         ((X, Z * cfg.pair, C), F32),
         ((X, 4, H, C), BF),
@@ -499,6 +507,7 @@
         ((Z, cfg.pad, cfg.main), BF),
         ((J, CORES, cfg.pad, C), F32),
         ((cfg.pad, C), F32),
+        ((cfg.own, C), F32),
         ((B, D), F32),
         ((2, Y - 1, B // 2, D), BF),
         ((2, Y - 1, B // 2, D), BF),
@@ -507,7 +516,7 @@
     one = ()
     sems = [
         one, one, one, (5,), one, (5,),
-        one, (F,), one, (F,), one, (F,), one, one,
+        one, (F,), one, (F,), one, (F,), one, (F,),
         one, (X,), one, (4,), one, one, (J, CORES), one, one,
         one, (2,), one, (2,),
     ]
@@ -515,7 +524,7 @@
         functools.partial(kernel, cfg),
         out_shape=(jax.ShapeDtypeStruct((R, D), BF), jax.ShapeDtypeStruct((cfg.own, C), F32)),
         in_specs=[pl.BlockSpec(memory_space=pltpu.SMEM), vmem, hbm, vmem, vmem, vmem, hbm],
-        out_specs=(hbm, vmem),
+        out_specs=(hbm, hbm),
         scratch_shapes=[pltpu.VMEM(shape, kind) for shape, kind in buffers]
         + [sem(n) for n in sems]
         + [pltpu.SemaphoreType.REGULAR, sem((2,)), sem(one)],

time: 72.5 us -> 71.6 us (0.988)
  Pallas kernels: 71 us -> 70.1 us
    pallas_call x1, Pallas kernels: 68.9 us -> 68 us  [module(): pl.pallas_call(functools.partial(kernel, cfg), out_shape=(jax.ShapeDtypeS...]
where the time goes in v9:
time: 71.6 us; the launch traced here: 71.4 us
  Pallas kernels  70.1 us (98%)
  between operations  1.29 us (2%)
    pallas_call x1, Pallas kernels, module(): pl.pallas_call(functools.partial(kernel, cfg), out_shape=(jax.ShapeDtypeS...  68 us
    pallas_call x1, Pallas kernels, module(): pl.pallas_call(functools.partial(place_results, U), out_shape=(jax.ShapeD...  2.07 us

profile of v9, /device:TPU:1, one launch (start us, length us, event | category | flops | bytes accessed | tf_op | source)
XLA Modules:
  0.0 71.4 jit_solution(13998437868027953706)
XLA Ops:
  1.3 68.0 %shard_map.102 = (bf16[256,1536]{1,0:T(8,128)(2,1)}, f32[12,576]{1,0:T(8,128)}) custom-call(s32[1]{0:T(128)S(6)} %copy.11.lengths, s32[1,256]{1,0:T(1,128)} %send_order.1, bf16[256,1536]{1,0:T(8,128)(2,1)} %frames_all.1, bf16[12,192]{1,0:T(8,128)(2,1)} %value_w.1, bf16[12,192]{1,0:T(8,128)(2,1)} %gate_w.1, bf16[12,192]{1,0:T(8,128)(2,1)} %down_w.1, ...), custom_call_target="tpu_custom_call" | custom-call | tf_op jit(solution)/shard_map/pallas_call | solution.py:523
  69.3 2.1 %shard_map.103 = (bf16[256,1536]{1,0:T(8,128)(2,1)}, f32[12,192]{1,0:T(8,128)}, f32[12,192]{1,0:T(8,128)}, f32[12,192]{1,0:T(8,128)}) custom-call(bf16[256,1536]{1,0:T(8,128)(2,1)} %get-tuple-element.6.branch_in, f32[12,576]{1,0:T(8,128)} %get-tuple-element.7.owned_in), custom_call_target="tpu_custom_call" | custom-call | tf_op jit(solution)/shard_map/pallas_call | solution.py:535

commit v10 on v9

--- a/solution.py
+++ b/solution.py
@@ -327,7 +327,7 @@
             [rows_of(block.at[o], (half * (Z // 2) + r + 4 * j) * Q, Q, 8)[...] for j in range(J)], axis=0
         )
 
-    for o in (2, 1, 3, 0):
+    def gradients(o):
         cols = pl.ds(pl.multiple_of(mod(x + o, X) * span, 128), span)
         block[o] = jnp.concatenate(
             [contract_rows(normed[:, cols], d_both), contract_rows(cot[:, cols], glu)], axis=1
@@ -336,34 +336,11 @@
             pair_out[o, i] = chunk(o, other, a).astype(BF)
         send(pair_out.at[o], pair_in.at[o], s_pair, r_pair.at[o], sibling)
 
+    for o in (2, 1, 3):
+        gradients(o)
+
     B = cfg.yrow
     half_b = B // 2
-
-    def gather(h):
-        drain(r_y.at[h], y_in.at[h])
-        lines = y_own[h * half_b : (h + 1) * half_b, :]
-        for k in range(Y - 1):
-            lines = lines + y_in[h, k].astype(F32)
-        ref = rows_of(result, y * B + h * half_b, half_b)
-        ref[...] = lines.astype(BF)
-        for d in (2, 1, 3):
-            send(ref, ref, s_yg, r_yg.at[h], at_y(d))
-
-    def put_out(h):
-        drain(r_yg.at[h], result.at[0 : (Y - 1) * half_b])
-        for i in range(Y):
-            lo = i * B + h * half_b
-            pltpu.make_async_copy(
-                result.at[lo : lo + half_b], branch.at[lo : lo + half_b], s_put
-            ).start()
-
-    def to_x(i, o):
-        x_out[i, o - 1] = (chunk(o, core, steps[i]) + pair_in[o, i].astype(F32)).astype(BF)
-        send(x_out.at[i, o - 1], x_in.at[i, o - 1], s_x, r_x.at[i], at_x(o))
-
-    for o in (2, 1, 3):
-        drain(r_pair.at[o], pair_in.at[o])
-        to_x(0, o)
 
     glu_rows[...] = dot(back, glu).astype(BF)
     for d in (2, 1, 3):
@@ -375,6 +352,34 @@
         for d in (2, 1, 3):
             send(y_out.at[h, d - 1], y_in.at[h, d - 1], s_y, r_y.at[h], at_y(d))
     y_own[...] = contract_cols(rows_of(glu_rows, y * B, B)[...], weights[:, 2 * U : 3 * U])
+
+    gradients(0)
+
+    def gather(h):
+        drain(r_y.at[h], y_in.at[h])
+        lines = y_own[h * half_b : (h + 1) * half_b, :]
+        for k in range(Y - 1):
+            lines = lines + y_in[h, k].astype(F32)
+        ref = rows_of(result, y * B + h * half_b, half_b)
+        ref[...] = lines.astype(BF)
+        for d in (2, 1, 3):
+            send(ref, ref, s_yg, r_yg.at[h], at_y(d))
+
+    def put_out(h):
+        drain(r_yg.at[h], result.at[0 : (Y - 1) * half_b])
+        for i in range(Y):
+            lo = i * B + h * half_b
+            pltpu.make_async_copy(
+                result.at[lo : lo + half_b], branch.at[lo : lo + half_b], s_put
+            ).start()
+
+    def to_x(i, o):
+        x_out[i, o - 1] = (chunk(o, core, steps[i]) + pair_in[o, i].astype(F32)).astype(BF)
+        send(x_out.at[i, o - 1], x_in.at[i, o - 1], s_x, r_x.at[i], at_x(o))
+
+    for o in (2, 1, 3):
+        drain(r_pair.at[o], pair_in.at[o])
+        to_x(0, o)
 
     for i in range(1, 4):
         for o in (2, 1, 3):

time: 71.6 us -> 71.3 us (level)
  no operation moved by 1% of the time
where the time goes in v10:
time: 71.3 us; the launch traced here: 71.1 us
  Pallas kernels  69.8 us (98%)
  between operations  1.29 us (2%)
    pallas_call x1, Pallas kernels, module(): pl.pallas_call(functools.partial(kernel, cfg), out_shape=(jax.ShapeDtypeS...  67.7 us
    pallas_call x1, Pallas kernels, module(): pl.pallas_call(functools.partial(place_results, U), out_shape=(jax.ShapeD...  2.07 us

profile of v10, /device:TPU:1, one launch (start us, length us, event | category | flops | bytes accessed | tf_op | source)
XLA Modules:
  0.0 71.1 jit_solution(8477753654310074731)
XLA Ops:
  1.3 67.7 %shard_map.102 = (bf16[256,1536]{1,0:T(8,128)(2,1)}, f32[12,576]{1,0:T(8,128)}) custom-call(s32[1]{0:T(128)S(6)} %copy.11.lengths, s32[1,256]{1,0:T(1,128)} %send_order.1, bf16[256,1536]{1,0:T(8,128)(2,1)} %frames_all.1, bf16[12,192]{1,0:T(8,128)(2,1)} %value_w.1, bf16[12,192]{1,0:T(8,128)(2,1)} %gate_w.1, bf16[12,192]{1,0:T(8,128)(2,1)} %down_w.1, ...), custom_call_target="tpu_custom_call" | custom-call | tf_op jit(solution)/shard_map/pallas_call | solution.py:528
  69.0 2.1 %shard_map.103 = (bf16[256,1536]{1,0:T(8,128)(2,1)}, f32[12,192]{1,0:T(8,128)}, f32[12,192]{1,0:T(8,128)}, f32[12,192]{1,0:T(8,128)}) custom-call(bf16[256,1536]{1,0:T(8,128)(2,1)} %get-tuple-element.6.branch_in, f32[12,576]{1,0:T(8,128)} %get-tuple-element.7.owned_in), custom_call_target="tpu_custom_call" | custom-call | tf_op jit(solution)/shard_map/pallas_call | solution.py:540

commit v11 on v9

--- a/solution.py
+++ b/solution.py
@@ -96,7 +96,7 @@
     lengths, send_order, frames_all, value_w, gate_w, down_w, cotangent_all,
     branch, owned,
     frames, cotangent, out1, in1, out2, moved, normed, cot, glu_rows,
-    shards, w_own, w_sib, staged, weights,
+    shards, w_own, w_sib, staged, weights, down,
     block, pair_out, pair_in, x_out, x_in, z_out, z_in, acc, final, last,
     y_own, y_out, y_in, result,
     s_a1, r_a1, s_a2, r_a2, s_ag, r_ag,
@@ -144,8 +144,10 @@
         return ref.at[pl.ds(pl.multiple_of(start, step), size)]
 
     barrier = pltpu.get_barrier_semaphore()
-    partners = [at_g(mod(g + o, G)) for o in range(1, G)]
-    partners += [at_z(o * s) for o in range(1, 5) for s in (1, -1)]
+    around = (4, 5, 2, 3, 6, 7, 1)
+    partners = [at_z(o * s) for o in (4, 3) for s in (1, -1)]
+    partners += [at_g(mod(g + o, G)) for o in around]
+    partners += [at_z(o * s) for o in (2, 1) for s in (1, -1)]
     partners += [at_y(o) for o in range(1, Y)]
     for who in partners:
         pl.semaphore_signal(barrier, inc=1, device_id=who, device_id_type=pl.DeviceIdType.MESH)
@@ -173,7 +175,7 @@
     for o in (4, -4):
         pl.semaphore_signal(relay, inc=1, device_id=at_z(o), device_id_type=pl.DeviceIdType.MESH)
 
-    for o in range(1, G):
+    for o in around:
         t = mod(g + o, G)
         send(
             rows_of(out1, t * cfg.grow, cfg.grow), rows_of(in1, g * cfg.grow, cfg.grow),
@@ -303,13 +305,14 @@
     normalize(2)
     put_weights(3)
     put_weights(2)
-    weights[...] = staged[...].astype(BF)
-
-    dglu = dot(cot[...], weights[:, 2 * U : 3 * U])
+    weights[...] = staged[:, : 2 * U].astype(BF)
+
     normalize(3)
     normalize(4)
 
-    both = dot(normed[...], weights[:, : 2 * U])
+    both = dot(normed[...], weights[...])
+    down[...] = staged[:, 2 * U :].astype(BF)
+    dglu = dot(cot[...], down[...])
     value, gate = both[:, :U], both[:, U : 2 * U]
     sig = jax.nn.sigmoid(gate)
     glu = (value * sig).astype(BF)
@@ -368,13 +371,13 @@
     glu_rows[...] = dot(back, glu).astype(BF)
     for d in (2, 1, 3):
         some = rows_of(glu_rows, mod(y + d, Y) * B, B)[...]
-        theirs = contract_cols(some, weights[:, 2 * U : 3 * U]).astype(BF)
+        theirs = contract_cols(some, down[...]).astype(BF)
         for h in range(2):
             y_out[h, d - 1] = theirs[h * half_b : (h + 1) * half_b]
     for h in range(2):
         for d in (2, 1, 3):
             send(y_out.at[h, d - 1], y_in.at[h, d - 1], s_y, r_y.at[h], at_y(d))
-    y_own[...] = contract_cols(rows_of(glu_rows, y * B, B)[...], weights[:, 2 * U : 3 * U])
+    y_own[...] = contract_cols(rows_of(glu_rows, y * B, B)[...], down[...])
 
     for i in range(1, 4):
         for o in (2, 1, 3):
@@ -497,7 +500,8 @@
         ((F, X, cfg.comb, C), BF),
         ((F, X, cfg.comb, C), BF),
         ((D, C), F32),
-        ((D, C), BF),
+        ((D, 2 * U), BF),
+        ((D, U), BF),
         ((X, Z * cfg.pair, C), F32),
         ((X, 4, H, C), BF),
         ((X, 4, H, C), BF),

time: 71.6 us -> 71.6 us (level)
  no operation moved by 1% of the time
where the time goes in v11:
time: 71.6 us; the launch traced here: 71.4 us
  Pallas kernels  70.1 us (98%)
  between operations  1.29 us (2%)
    pallas_call x1, Pallas kernels, module(): pl.pallas_call(functools.partial(kernel, cfg), out_shape=(jax.ShapeDtypeS...  68 us
    pallas_call x1, Pallas kernels, module(): pl.pallas_call(functools.partial(place_results, U), out_shape=(jax.ShapeD...  2.07 us

profile of v11, /device:TPU:1, one launch (start us, length us, event | category | flops | bytes accessed | tf_op | source)
XLA Modules:
  0.0 71.4 jit_solution(16721051569466413677)
XLA Ops:
  1.3 68.0 %shard_map.102 = (bf16[256,1536]{1,0:T(8,128)(2,1)}, f32[12,576]{1,0:T(8,128)}) custom-call(s32[1]{0:T(128)S(6)} %copy.11.lengths, s32[1,256]{1,0:T(1,128)} %send_order.1, bf16[256,1536]{1,0:T(8,128)(2,1)} %frames_all.1, bf16[12,192]{1,0:T(8,128)(2,1)} %value_w.1, bf16[12,192]{1,0:T(8,128)(2,1)} %gate_w.1, bf16[12,192]{1,0:T(8,128)(2,1)} %down_w.1, ...), custom_call_target="tpu_custom_call" | custom-call | tf_op jit(solution)/shard_map/pallas_call | solution.py:527
  69.3 2.1 %shard_map.103 = (bf16[256,1536]{1,0:T(8,128)(2,1)}, f32[12,192]{1,0:T(8,128)}, f32[12,192]{1,0:T(8,128)}, f32[12,192]{1,0:T(8,128)}) custom-call(bf16[256,1536]{1,0:T(8,128)(2,1)} %get-tuple-element.6.branch_in, f32[12,576]{1,0:T(8,128)} %get-tuple-element.7.owned_in), custom_call_target="tpu_custom_call" | custom-call | tf_op jit(solution)/shard_map/pallas_call | solution.py:539

commit v12 on v11

--- a/solution.py
+++ b/solution.py
@@ -175,6 +175,21 @@
     for o in (4, -4):
         pl.semaphore_signal(relay, inc=1, device_id=at_z(o), device_id_type=pl.DeviceIdType.MESH)
 
+    near = (1, -1, 2)
+
+    def pass_near(f):
+        ref = shards.at[f, cfg.pad : 2 * cfg.pad]
+        for a in near:
+            lo = (a + 1) * cfg.pad
+            send(ref, shards.at[f, lo : lo + cfg.pad], s_wn, r_wn.at[f], at_z(a))
+
+    def pass_far(f):
+        send(mine, shards.at[f, cfg.pad : 2 * cfg.pad], s_wf, r_wf.at[f], at_z(4 * f))
+
+    pass_near(0)
+    for f in range(1, F):
+        if 4 * f != Z // 2:
+            pass_far(f)
     for o in around:
         t = mod(g + o, G)
         send(
@@ -183,21 +198,6 @@
         )
     rows_of(in1, g * cfg.grow, cfg.grow)[...] = rows_of(out1, g * cfg.grow, cfg.grow)[...]
 
-    near = (1, -1, 2)
-
-    def pass_near(f):
-        ref = shards.at[f, cfg.pad : 2 * cfg.pad]
-        for a in near:
-            lo = (a + 1) * cfg.pad
-            send(ref, shards.at[f, lo : lo + cfg.pad], s_wn, r_wn.at[f], at_z(a))
-
-    def pass_far(f):
-        send(mine, shards.at[f, cfg.pad : 2 * cfg.pad], s_wf, r_wf.at[f], at_z(4 * f))
-
-    pass_near(0)
-    for f in range(1, F):
-        if 4 * f != Z // 2:
-            pass_far(f)
     pl.semaphore_wait(relay, 2)
     pass_far(F // 2)
 
@@ -297,8 +297,8 @@
     normalize(0)
     share(3)
     hand_on(3)
+    hand_on(2)
     share(4)
-    hand_on(2)
     normalize(1)
     put_weights(0)
     put_weights(1)

time: 71.6 us -> 71.5 us (level)
  no operation moved by 1% of the time
where the time goes in v12:
time: 71.5 us; the launch traced here: 71.3 us
  Pallas kernels  70 us (98%)
  between operations  1.29 us (2%)
    pallas_call x1, Pallas kernels, module(): pl.pallas_call(functools.partial(kernel, cfg), out_shape=(jax.ShapeDtypeS...  67.9 us
    pallas_call x1, Pallas kernels, module(): pl.pallas_call(functools.partial(place_results, U), out_shape=(jax.ShapeD...  2.07 us

profile of v12, /device:TPU:1, one launch (start us, length us, event | category | flops | bytes accessed | tf_op | source)
XLA Modules:
  0.0 71.3 jit_solution(10180130735288982846)
XLA Ops:
  1.3 67.9 %shard_map.102 = (bf16[256,1536]{1,0:T(8,128)(2,1)}, f32[12,576]{1,0:T(8,128)}) custom-call(s32[1]{0:T(128)S(6)} %copy.11.lengths, s32[1,256]{1,0:T(1,128)} %send_order.1, bf16[256,1536]{1,0:T(8,128)(2,1)} %frames_all.1, bf16[12,192]{1,0:T(8,128)(2,1)} %value_w.1, bf16[12,192]{1,0:T(8,128)(2,1)} %gate_w.1, bf16[12,192]{1,0:T(8,128)(2,1)} %down_w.1, ...), custom_call_target="tpu_custom_call" | custom-call | tf_op jit(solution)/shard_map/pallas_call | solution.py:527
  69.2 2.1 %shard_map.103 = (bf16[256,1536]{1,0:T(8,128)(2,1)}, f32[12,192]{1,0:T(8,128)}, f32[12,192]{1,0:T(8,128)}, f32[12,192]{1,0:T(8,128)}) custom-call(bf16[256,1536]{1,0:T(8,128)(2,1)} %get-tuple-element.6.branch_in, f32[12,576]{1,0:T(8,128)} %get-tuple-element.7.owned_in), custom_call_target="tpu_custom_call" | custom-call | tf_op jit(solution)/shard_map/pallas_call | solution.py:539

commit v13 on v11

--- a/solution.py
+++ b/solution.py
@@ -201,6 +201,16 @@
     pl.semaphore_wait(relay, 2)
     pass_far(F // 2)
 
+    where = lax.div(place, cfg.zrow)
+    away = jnp.where(lax.rem(where, 2) == 1, lax.div(where + 1, 2), lax.rem(Z - lax.div(where, 2), Z))
+    k_at, g_at = lax.rem(place, cap), lax.rem(lax.div(place, cap), G)
+    natural = (
+        (lax.div(g_at, CORES) * Z + lax.rem(z + away, Z)) * CORES + lax.rem(g_at, CORES)
+    ) * cap + k_at
+    back = onehot(row == natural)
+    get_cotangent.wait()
+    cot[...] = contract_rows(back, cotangent[...]).astype(BF)
+
     to_new = (z_of * G + g_of) * cap + k_of
     drain(r_a1, in1.at[0 : (G - 1) * cfg.grow])
     out2[...] = dot(onehot(row == to_new), in1[...]).astype(BF)
@@ -239,16 +249,6 @@
         drain(r_wf.at[f], shards.at[f, cfg.pad : 2 * cfg.pad])
         pass_near(f)
     to_z((2, 3, 4))
-
-    where = lax.div(place, cfg.zrow)
-    away = jnp.where(lax.rem(where, 2) == 1, lax.div(where + 1, 2), lax.rem(Z - lax.div(where, 2), Z))
-    k_at, g_at = lax.rem(place, cap), lax.rem(lax.div(place, cap), G)
-    natural = (
-        (lax.div(g_at, CORES) * Z + lax.rem(z + away, Z)) * CORES + lax.rem(g_at, CORES)
-    ) * cap + k_at
-    back = onehot(row == natural)
-    get_cotangent.wait()
-    cot[...] = contract_rows(back, cotangent[...]).astype(BF)
 
     def share(j):
         lo, hi = bounds[j]

time: 71.6 us -> 71.4 us (level)
  no operation moved by 1% of the time
where the time goes in v13:
time: 71.4 us; the launch traced here: 71.2 us
  Pallas kernels  69.9 us (98%)
  between operations  1.29 us (2%)
    pallas_call x1, Pallas kernels, module(): pl.pallas_call(functools.partial(kernel, cfg), out_shape=(jax.ShapeDtypeS...  67.8 us
    pallas_call x1, Pallas kernels, module(): pl.pallas_call(functools.partial(place_results, U), out_shape=(jax.ShapeD...  2.07 us

profile of v13, /device:TPU:1, one launch (start us, length us, event | category | flops | bytes accessed | tf_op | source)
XLA Modules:
  0.0 71.2 jit_solution(4874806903409854503)
XLA Ops:
  1.3 67.8 %shard_map.102 = (bf16[256,1536]{1,0:T(8,128)(2,1)}, f32[12,576]{1,0:T(8,128)}) custom-call(s32[1]{0:T(128)S(6)} %copy.11.lengths, s32[1,256]{1,0:T(1,128)} %send_order.1, bf16[256,1536]{1,0:T(8,128)(2,1)} %frames_all.1, bf16[12,192]{1,0:T(8,128)(2,1)} %value_w.1, bf16[12,192]{1,0:T(8,128)(2,1)} %gate_w.1, bf16[12,192]{1,0:T(8,128)(2,1)} %down_w.1, ...), custom_call_target="tpu_custom_call" | custom-call | tf_op jit(solution)/shard_map/pallas_call | solution.py:527
  69.1 2.1 %shard_map.103 = (bf16[256,1536]{1,0:T(8,128)(2,1)}, f32[12,192]{1,0:T(8,128)}, f32[12,192]{1,0:T(8,128)}, f32[12,192]{1,0:T(8,128)}) custom-call(bf16[256,1536]{1,0:T(8,128)(2,1)} %get-tuple-element.6.branch_in, f32[12,576]{1,0:T(8,128)} %get-tuple-element.7.owned_in), custom_call_target="tpu_custom_call" | custom-call | tf_op jit(solution)/shard_map/pallas_call | solution.py:539
